TPU v7x, 256 devices: a whole 4x4x8 slice. The times are simulated.
256 devices in a mesh: dp: 32 (over y, z), cent: 8 (over x, core).
Axes of the slice: x: 4, y: 4, z: 8, core: 2. Of those that a mesh axis runs over, the one named last changes fastest.
Arguments:
- stream: bfloat16 [65536, 768], P('dp'), may hold values from -6 to 6
- sample_index: int32 [32768], P('dp'), may hold values from 0 to 2047
- centroids: float32 [16384, 768], P(('cent', 'dp')), may hold values from -6 to 6
- first_moment: float32 [16384, 768], P(('cent', 'dp')), may hold values from -3 to 3
- second_moment: float32 [16384, 768], P(('cent', 'dp')), may hold values from 0.01 to 1
Outputs:
- new_centroids: float32 [16384, 768], P(('cent', 'dp'))
- new_first: float32 [16384, 768], P(('cent', 'dp'))
- new_second: float32 [16384, 768], P(('cent', 'dp'))
All inputs are finite; a program needn't handle non-finite values.
Results may differ from a plain program's by a relative error of at most 0.0003.
Values may be sent and summed in bfloat16 or wider, within the bound.
A program may use at most 64 MiB of HBM per device.

v0:
```python
import math

import jax
import jax.numpy as jnp
from jax import lax
from jax.sharding import PartitionSpec as P

KB = 16384
ITERS = 3


temper = 2.0
beta_one = 0.9
beta_two = 0.99
step_rate = 0.05
epsilon = 1e-08


def per_device(stream, sample_index, centroids, first_moment, second_moment):
    embedded = stream[sample_index]
    local_rows = embedded.shape[0]
    total_rows = local_rows * lax.axis_size("dp")
    balance = math.log(total_rows / KB)
    rounded = centroids.astype(jnp.bfloat16)
    shard_piece = lax.all_gather(rounded, "dp", axis=0, tiled=True)
    squares = jnp.sum(shard_piece.astype(jnp.float32) ** 2, axis=1)
    product = lax.dot_general(
        embedded, shard_piece, (((1,), (1,)), ((), ())), preferred_element_type=jnp.float32
    )
    logits = (2.0 * product - squares[None, :]) / temper

    def row_potential(column_pot):
        shifted = logits + column_pot[None, :]
        highest = jnp.max(shifted, axis=1)
        summed = jnp.sum(jnp.exp(shifted - highest[:, None]), axis=1)
        overall = lax.pmax(highest, "cent")
        summed = lax.psum(summed * jnp.exp(highest - overall), "cent")
        highest = overall
        return -(highest + jnp.log(summed))

    column_pot = jnp.zeros((logits.shape[1],), jnp.float32)
    for sweep_index in range(ITERS):
        column_shifted = logits + row_potential(column_pot)[:, None]
        column_highest = jnp.max(column_shifted, axis=0)
        column_summed = jnp.sum(jnp.exp(column_shifted - column_highest[None, :]), axis=0)
        column_overall = lax.pmax(column_highest, "dp")
        column_summed = lax.psum(column_summed * jnp.exp(column_highest - column_overall), "dp")
        column_highest = column_overall
        column_pot = balance - (column_highest + jnp.log(column_summed))
    row_pot = row_potential(column_pot)
    transport = jnp.exp(logits + row_pot[:, None] + column_pot[None, :]).astype(jnp.bfloat16)
    weighted = lax.dot_general(
        transport, embedded, (((0,), (0,)), ((), ())), preferred_element_type=jnp.float32
    )
    weight_mass = jnp.sum(transport.astype(jnp.float32), axis=0)
    weighted, weight_mass = lax.psum((weighted, weight_mass), "dp")
    owned_rows = centroids.shape[0]
    offset_rows = lax.axis_index("dp") * owned_rows
    weighted = lax.dynamic_slice_in_dim(weighted, offset_rows, owned_rows, 0)
    weight_mass = lax.dynamic_slice_in_dim(weight_mass, offset_rows, owned_rows, 0)
    gradient = (weight_mass[:, None] * centroids - weighted) * (KB / total_rows)
    new_first = beta_one * first_moment + (1.0 - beta_one) * gradient
    new_second = beta_two * second_moment + (1.0 - beta_two) * gradient * gradient
    new_centroids = centroids - step_rate * new_first / (jnp.sqrt(new_second) + epsilon)
    return (new_centroids, new_first, new_second)


def solution(mesh):
    return jax.shard_map(
        per_device,
        mesh=mesh,
        in_specs=(
            P("dp", None),
            P("dp"),
            P(("cent", "dp"), None),
            P(("cent", "dp"), None),
            P(("cent", "dp"), None),
        ),
        out_specs=(P(("cent", "dp"), None), P(("cent", "dp"), None), P(("cent", "dp"), None)),
        check_vma=False,
    )
```

profile of v0, /device:TPU:8, one launch (start us, length us, event | category | flops | bytes accessed | tf_op | source)
XLA Modules:
  0.0 888.4 jit_solution(12046903474257052355)
XLA Ops:
  7.2 0.0 copy-start
  7.2 0.0 all-gather.2.cloned.1.call-start
  7.2 1.7 convert_element_type.12
  9.0 0.0 all-gather.2.cloned.1.call-update
  9.0 0.0 all-reduce.2.cloned.1.call-start
  9.0 0.7 fusion
  9.7 0.0 copy-done
  9.7 5.2 gather_fusion
  15.0 77.8 %all-gather.2.cloned.1.call-done = bf16[2048,768]{1,0:T(8,128)(2,1)} async-done(((bf16[64,768]{1,0:T(8,128)(2,1)}), bf16[2048,768]{1,0:T(8,128)(2,1)}) %all-gather.2.cloned.1.call-update) | async-done | bytes 3145744 | tf_op jit(solution)/shard_map/all_gather | solution.py:25
  92.8 2.6 multiply_reduce_fusion
  95.4 9.1 %fusion.2 = (f32[1024]{0:T(1024)S(1)}, f32[1024,2048]{1,0:T(8,128)}) fusion(f32[2048]{0:T(1024)S(1)} %multiply_reduce_fusion, bf16[1024,768]{1,0:T(8,128)(2,1)} %gather_fusion, bf16[2048,768]{1,0:T(8,128)(2,1)} %all-gather.2.cloned.1.call-done), kind=kOutput, calls=%fused_computation.39 | convolution fusion | flops 3229613056 | bytes 13119488 | tf_op jit(solution)/shard_map/dot_general | solution.py:27
  104.4 12.4 %pmax.49 = f32[1024]{0:T(1024)S(1)} all-reduce(f32[1024]{0:T(1024)S(1)} %get-tuple-element.6), channel_id=1, replica_groups=mesh['dp'=32,'cent'=8] {'cent'}, use_global_device_ids=true, to_apply=%region_2.0 | all-reduce | flops 1024 | bytes 8192 | tf_op jit(solution)/shard_map/pmax | solution.py:36
  116.8 4.6 exponential_reduce_fusion.6
  121.5 12.4 %psum.63 = f32[1024]{0:T(1024)S(1)} all-reduce(f32[1024]{0:T(1024)S(1)} %exponential_multiply_fusion.6), channel_id=1, replica_groups=mesh['dp'=32,'cent'=8] {'cent'}, use_global_device_ids=true, to_apply=%region_4.0 | all-reduce | flops 1024 | bytes 8192 | tf_op jit(solution)/shard_map/psum | solution.py:37
  133.9 4.0 add_reduce_fusion.5
  137.9 4.3 exponential_reduce_fusion.5
  142.2 64.0 %pmax.50 = f32[2048]{0:T(1024)S(1)} all-reduce(f32[2048]{0:T(1024)S(1)} %add_reduce_fusion.5), channel_id=1, replica_groups=mesh['dp'=32,'cent'=8] {'dp'}, use_global_device_ids=true, to_apply=%region_6.0 | all-reduce | flops 2048 | bytes 16384 | tf_op jit(solution)/shard_map/pmax | solution.py:46
  206.2 68.6 %psum.64 = f32[2048]{0:T(1024)S(1)} all-reduce(f32[2048]{0:T(1024)S(1)} %exponential_multiply_fusion.2), channel_id=1, replica_groups=mesh['dp'=32,'cent'=8] {'dp'}, use_global_device_ids=true, to_apply=%region_8.0 | all-reduce | flops 2048 | bytes 16384 | tf_op jit(solution)/shard_map/psum | solution.py:47
  274.9 4.0 add_reduce_fusion.4
  278.9 4.4 exponential_reduce_fusion.4
  283.3 12.4 %pmax.51 = f32[1024]{0:T(1024)S(1)} all-reduce(f32[1024]{0:T(1024)S(1)} %add_reduce_fusion.4), channel_id=1, replica_groups=mesh['dp'=32,'cent'=8] {'cent'}, use_global_device_ids=true, to_apply=%region_10.0 | all-reduce | flops 1024 | bytes 8192 | tf_op jit(solution)/shard_map/pmax | solution.py:36
  295.8 12.4 %psum.65 = f32[1024]{0:T(1024)S(1)} all-reduce(f32[1024]{0:T(1024)S(1)} %exponential_multiply_fusion.5), channel_id=1, replica_groups=mesh['dp'=32,'cent'=8] {'cent'}, use_global_device_ids=true, to_apply=%region_12.0 | all-reduce | flops 1024 | bytes 8192 | tf_op jit(solution)/shard_map/psum | solution.py:37
  308.2 4.0 add_reduce_fusion.3
  312.2 4.3 exponential_reduce_fusion.3
  316.5 72.7 %pmax.52 = f32[2048]{0:T(1024)S(1)} all-reduce(f32[2048]{0:T(1024)S(1)} %add_reduce_fusion.3), channel_id=1, replica_groups=mesh['dp'=32,'cent'=8] {'dp'}, use_global_device_ids=true, to_apply=%region_14.0 | all-reduce | flops 2048 | bytes 16384 | tf_op jit(solution)/shard_map/pmax | solution.py:46
  389.2 70.8 %psum.66 = f32[2048]{0:T(1024)S(1)} all-reduce(f32[2048]{0:T(1024)S(1)} %exponential_multiply_fusion.1), channel_id=1, replica_groups=mesh['dp'=32,'cent'=8] {'dp'}, use_global_device_ids=true, to_apply=%region_16.0 | all-reduce | flops 2048 | bytes 16384 | tf_op jit(solution)/shard_map/psum | solution.py:47
  460.1 4.0 add_reduce_fusion.2
  464.1 4.4 exponential_reduce_fusion.2
  468.5 12.4 %pmax.53 = f32[1024]{0:T(1024)S(1)} all-reduce(f32[1024]{0:T(1024)S(1)} %add_reduce_fusion.2), channel_id=1, replica_groups=mesh['dp'=32,'cent'=8] {'cent'}, use_global_device_ids=true, to_apply=%region_18.0 | all-reduce | flops 1024 | bytes 8192 | tf_op jit(solution)/shard_map/pmax | solution.py:36
  480.9 12.4 %psum.67 = f32[1024]{0:T(1024)S(1)} all-reduce(f32[1024]{0:T(1024)S(1)} %exponential_multiply_fusion.4), channel_id=1, replica_groups=mesh['dp'=32,'cent'=8] {'cent'}, use_global_device_ids=true, to_apply=%region_20.0 | all-reduce | flops 1024 | bytes 8192 | tf_op jit(solution)/shard_map/psum | solution.py:37
  493.4 4.0 add_reduce_fusion.1
  497.4 4.3 exponential_reduce_fusion.1
  501.7 72.7 %pmax.54 = f32[2048]{0:T(1024)S(1)} all-reduce(f32[2048]{0:T(1024)S(1)} %add_reduce_fusion.1), channel_id=1, replica_groups=mesh['dp'=32,'cent'=8] {'dp'}, use_global_device_ids=true, to_apply=%region_22.0 | all-reduce | flops 2048 | bytes 16384 | tf_op jit(solution)/shard_map/pmax | solution.py:46
  574.5 70.6 %psum.68 = f32[2048]{0:T(1024)S(1)} all-reduce(f32[2048]{0:T(1024)S(1)} %exponential_multiply_fusion), channel_id=1, replica_groups=mesh['dp'=32,'cent'=8] {'dp'}, use_global_device_ids=true, to_apply=%region_24.0 | all-reduce | flops 2048 | bytes 16384 | tf_op jit(solution)/shard_map/psum | solution.py:47
  645.1 4.0 add_reduce_fusion
  649.1 4.4 exponential_reduce_fusion
  653.5 12.4 %pmax.55 = f32[1024]{0:T(1024)S(1)} all-reduce(f32[1024]{0:T(1024)S(1)} %add_reduce_fusion), channel_id=1, replica_groups=mesh['dp'=32,'cent'=8] {'cent'}, use_global_device_ids=true, to_apply=%region_26.0 | all-reduce | flops 1024 | bytes 8192 | tf_op jit(solution)/shard_map/pmax | solution.py:36
  665.9 12.4 %psum.69 = f32[1024]{0:T(1024)S(1)} all-reduce(f32[1024]{0:T(1024)S(1)} %exponential_multiply_fusion.3), channel_id=1, replica_groups=mesh['dp'=32,'cent'=8] {'cent'}, use_global_device_ids=true, to_apply=%region_28.0 | all-reduce | flops 1024 | bytes 8192 | tf_op jit(solution)/shard_map/psum | solution.py:37
  678.4 0.6 copy-done.3
  679.0 10.4 %fusion.1 = f32[2048,768]{1,0:T(8,128)} fusion(bf16[1024,768]{1,0:T(8,128)(2,1)} %gather_fusion, f32[1024,2048]{1,0:T(8,128)} %get-tuple-element.7, f32[1024]{0:T(1024)S(1)} %add_negate_fusion, f32[2048]{0:T(1024)S(1)} %add_subtract_fusion), kind=kOutput, calls=%fused_computation.38 | convolution fusion | flops 3227516928 | bytes 16265216 | tf_op jit(solution)/shard_map/dot_general | solution.py:52
  689.3 0.0 all-reduce.2.cloned.1.call-update
  689.4 4.3 convert_reduce_fusion
  693.7 74.6 %psum.70 = f32[2048]{0:T(1024)S(1)} all-reduce(f32[2048]{0:T(1024)S(1)} %convert_reduce_fusion), channel_id=1, replica_groups=mesh['dp'=32,'cent'=8] {'dp'}, use_global_device_ids=true, to_apply=%region_30.0 | all-reduce | flops 2048 | bytes 16384 | tf_op jit(solution)/shard_map/psum | solution.py:56
  768.3 0.1 dynamic_slice.6
  768.4 111.2 %all-reduce.2.cloned.1.call-done = f32[2048,768]{1,0:T(8,128)} async-done(((f32[2048,768]{1,0:T(8,128)}), f32[2048,768]{1,0:T(8,128)}) %all-reduce.2.cloned.1.call-update) | async-done | bytes 6291472 | tf_op jit(solution)/shard_map/psum | solution.py:56
  879.6 0.0 copy-done.1
  879.6 0.0 copy-done.2
  879.6 2.0 divide_subtract_fusion
  (17 shorter events, 0.1 us)
Async XLA Ops:
  7.2 2.6 copy-start
  7.2 85.6 %all-gather.2.cloned.1.call-start = ((), (), s32[]{:S(2)}) async-start(), calls=%async_computation | async-start | bytes 3244032 | tf_op jit(solution)/shard_map/all_gather | solution.py:25
  9.0 870.6 %all-reduce.2.cloned.1.call-start = ((), (), s32[]{:S(2)}) async-start(), calls=%async_computation.1 | async-start | bytes 12582912 | tf_op jit(solution)/shard_map/psum | solution.py:56
  678.4 0.6 copy-start.3
  689.3 190.3 %copy-start.1 = (f32[64,768]{1,0:T(8,128)S(1)}, f32[64,768]{1,0:T(8,128)}, u32[]{:S(2)}) copy-start(f32[64,768]{1,0:T(8,128)} %param.7) | copy-start | bytes 589828
  689.3 190.3 %copy-start.2 = (f32[64,768]{1,0:T(8,128)S(1)}, f32[64,768]{1,0:T(8,128)}, u32[]{:S(2)}) copy-start(f32[64,768]{1,0:T(8,128)} %param.8) | copy-start | bytes 589828
Sparse Core Ops, SparseCore 0:
  11.2 81.5 all-gather.1
  689.5 190.0 all-reduce.1
where the time goes:
time: 890 us; the launch traced here: 888 us
  blocking collectives  594 us (67%)
  waiting for transfers between devices  189 us (21%)
  other arithmetic  66.1 us (7%)
  matrix products  19.4 us (2%)
  between operations  14.3 us (2%)
    psum x3, blocking collectives, per_device(): lax.psum(column_summed * jnp.exp(column_highest - column_overall), 'dp')  210 us
    pmax x3, blocking collectives, per_device(): column_overall = lax.pmax(column_highest, 'dp')  209 us
    psum x1, waiting for transfers between devices, per_device(): weighted, weight_mass = lax.psum((weighted, weight_mass), 'dp')  111 us
    all_gather x1, waiting for transfers between devices, per_device(): shard_piece = lax.all_gather(rounded, 'dp', axis=0, tiled=True)  77.8 us
    psum x1, blocking collectives, per_device(): weighted, weight_mass = lax.psum((weighted, weight_mass), 'dp')  74.6 us
    psum x4, blocking collectives, row_potential(): summed = lax.psum(summed * jnp.exp(highest - overall), 'cent')  49.7 us
    pmax x4, blocking collectives, row_potential(): overall = lax.pmax(highest, 'cent')  49.7 us
  transfers between devices with their start and end apart: 2, of which 2 were waited for; matrix products, arithmetic and copies ran while one was open for 1% of the time, Pallas kernels for 0%

commit v1 on v0

v1 whole, which is shorter than its diff:
```python
import functools
import math

import jax
import jax.numpy as jnp
from jax import lax
from jax.experimental import pallas as pl
from jax.experimental.pallas import tpu as pltpu
from jax.sharding import PartitionSpec as P

MESH = pl.DeviceIdType.MESH

KB = 16384
ROWS = 32768
NX, NY, NZ = 4, 4, 8
E = 768
OWN = 64
COLS = OWN * NZ
ND = 1024
BLK = 128
SLOTS = NY * ND // BLK
NR = SLOTS * BLK
STREAM = 2 * ND
BALANCE = math.log(ROWS / KB)
SUM_TYPE = jnp.float32
HALF = E // 2

beta_one = 0.9
beta_two = 0.99
step_rate = 0.05
epsilon = 1e-08


def pick(i, values):
    chosen = values[0]
    for k, value in enumerate(values[1:], 1):
        chosen = jnp.where(i == k, value, chosen)
    return chosen


def kernel(
    stream, idx, cent, grad,
    emb, piece, logits, transport, half_sq, col_part, col_part2, col_vec,
    row_vec, row_buf0, row_buf, row_sums, y_vec, y_buf0, y_buf, pot,
    col_send0, col_send, col_buf0, col_buf,
    partial, long_out, short_out, long_in, short_in,
    emb_send, emb_recv, sib_send, sib_recv, z_send, z_recv,
    row_send_sem, row_recv_sem, y_send_sem, y_recv_sem, col_send_sem, col_recv_sem,
    long_send_sem, long_recv_sem, short_send_sem, short_recv_sem,
):
    dp = lax.axis_index("dp")
    group = lax.axis_index("cent")
    y, z = dp // NZ, lax.rem(dp, NZ)
    x, core = group // 2, lax.rem(group, 2)

    def at_y(k):
        return {"dp": lax.rem(y + k + NY, NY) * NZ + z, "cent": group}

    def at_z(k):
        return {"dp": y * NZ + lax.rem(z + k + NZ, NZ), "cent": group}

    def at_x(k):
        return {"dp": dp, "cent": lax.rem(x + k + NX, NX) * 2 + core}

    def at_group(k):
        return {"dp": dp, "cent": lax.rem(group + k, 2 * NX)}

    sibling = {"dp": dp, "cent": x * 2 + 1 - core}

    barrier = pltpu.get_barrier_semaphore()
    for k in range(1, 2 * NX):
        pl.semaphore_signal(barrier, inc=1, device_id=at_group(k), device_id_type=MESH)
    for k in range(1, NY):
        pl.semaphore_signal(barrier, inc=1, device_id=at_y(k), device_id_type=MESH)
    for k in range(1, NZ):
        pl.semaphore_signal(barrier, inc=1, device_id=at_z(k), device_id_type=MESH)

    pending = []

    def send(src, dst, send_sem, recv_sem, device):
        copy = pltpu.make_async_remote_copy(
            src_ref=src, dst_ref=dst, send_sem=send_sem, recv_sem=recv_sem,
            device_id=device, device_id_type=MESH,
        )
        copy.start()
        pending.append(copy)

    def arrived(dst, recv_sem):
        pltpu.make_async_remote_copy(
            src_ref=dst, dst_ref=dst, send_sem=recv_sem, recv_sem=recv_sem,
            device_id=sibling, device_id_type=MESH,
        ).wait_recv()

    def slot_of(k, c, j):
        return lax.rem(y + k + NY, NY) * 8 + c * 4 + lax.rem(x + j, 4)

    def emb_at(slot, count=1):
        return emb.at[pl.ds(pl.multiple_of(slot * BLK, BLK), count * BLK), :]

    sends = [0]

    def send_block(slot, device):
        send(emb_at(slot), emb_at(slot), emb_send.at[sends[0]], emb_recv.at[slot], device)
        sends[0] += 1

    def wait_block(slot):
        arrived(emb_at(slot), emb_recv.at[slot])

    def piece_at(k):
        return piece.at[pl.ds(pl.multiple_of(lax.rem(z + k + NZ, NZ) * OWN, OWN), OWN), :]

    z_sends = [0]

    def send_piece(k, toward):
        owner = lax.rem(z + k + NZ, NZ)
        send(piece_at(k), piece_at(k), z_send.at[z_sends[0]], z_recv.at[owner], at_z(toward))
        z_sends[0] += 1

    def wait_piece(k):
        arrived(piece_at(k), z_recv.at[lax.rem(z + k + NZ, NZ)])

    def gather(j):
        quarter = lax.rem(x + j, 4)
        picked = idx[pl.ds(core * 4 + quarter, 1), :].astype(jnp.float32)
        column = jnp.broadcast_to(picked, (BLK, BLK)).T[:, :1]
        place = lax.broadcasted_iota(jnp.int32, (BLK, STREAM), 1).astype(jnp.float32)
        one_hot = jnp.where(place == column, 1.0, 0.0).astype(jnp.bfloat16)
        rows = jnp.dot(one_hot, stream[...], preferred_element_type=jnp.float32)
        slot = slot_of(0, core, j)
        emb[pl.ds(pl.multiple_of(slot * BLK, BLK), BLK), :] = rows.astype(jnp.bfloat16)
        return slot

    piece[pl.ds(pl.multiple_of(z * OWN, OWN), OWN), :] = cent[...].astype(jnp.bfloat16)
    first = gather(0)
    pl.semaphore_wait(barrier, 2 * NX + NY + NZ - 3)
    send_block(first, at_y(1))
    send_block(first, at_y(-1))
    send_piece(0, 1)
    send_piece(0, -1)
    second = gather(2)
    send_block(second, at_y(1))
    send_block(second, at_y(-1))
    gather(1)
    gather(3)
    own_first = y * 8 + core * 4
    send(emb_at(own_first, 4), emb_at(own_first, 4), sib_send, sib_recv, sibling)

    def on_piece(k, forward):
        wait_piece(k)
        if forward:
            send_piece(k, 1 if k < 0 else -1)

    def on_block(k, j, forward=(), spread=False):
        slot = slot_of(k, core, j)
        wait_block(slot)
        for toward in forward:
            send_block(slot, at_y(toward))
        if spread:
            send_block(slot, at_x(1))
            send_block(slot, at_x(-1))
        send_block(slot, sibling)

    def score(slot):
        lanes = pl.ds(pl.multiple_of(slot * BLK, BLK), BLK)
        rows = emb[pl.ds(pl.multiple_of(slot * BLK, BLK), BLK), :]
        product = lax.dot_general(
            piece[...], rows, (((1,), (1,)), ((), ())), preferred_element_type=jnp.float32
        )
        values = product - half_sq[...]
        logits[:, lanes] = values
        highest = jnp.max(values, axis=0, keepdims=True)
        row_vec[0:1, lanes] = highest
        row_vec[1:2, lanes] = jnp.sum(jnp.exp(values - highest), axis=0, keepdims=True)

    def score_all(offsets, c, wait):
        slots = [slot_of(k, c, j) for k, j in offsets]

        def body(i, carry):
            slot = pick(i, slots)
            if wait:
                wait_block(slot)
            score(slot)
            return carry

        lax.fori_loop(0, len(slots), body, 0)

    wave1 = [(-1, 0), (1, 0)]
    wave2 = [(2, 0), (-1, 1), (-1, 3), (1, 2)]
    wave3 = [(1, 1), (1, 3), (-1, 2), (2, 2)]
    wave4 = [(2, 1), (2, 3)]

    on_piece(-1, True)
    on_piece(1, True)
    on_block(-1, 0, forward=(1,), spread=True)
    on_block(1, 0, spread=True)
    on_piece(-2, True)
    on_piece(2, True)
    on_piece(-3, True)
    on_piece(3, False)
    on_block(2, 0, spread=True)
    on_block(1, 2, forward=(-1,))
    on_block(-1, 1)
    on_block(-1, 3)
    on_piece(-4, False)
    whole = piece[...].astype(jnp.float32)
    half_sq[...] = jnp.broadcast_to(
        0.5 * jnp.sum(whole * whole, axis=1, keepdims=True), (COLS, BLK)
    )
    score_all([(0, 0), (0, 1), (0, 2), (0, 3)], core, False)
    score_all(wave1, core, False)
    arrived(emb_at(y * 8 + (1 - core) * 4, 4), sib_recv)
    score_all([(0, 0), (0, 1), (0, 2), (0, 3)], 1 - core, False)
    score_all(wave1, 1 - core, True)
    score_all(wave2, core, False)
    for k, j in wave3:
        on_block(k, j)
    score_all(wave2, 1 - core, True)
    score_all(wave3, core, False)
    for k, j in wave4:
        on_block(k, j)
    score_all(wave3, 1 - core, True)
    score_all(wave4, core, False)
    score_all(wave4, 1 - core, True)

    def exchange_group(src, bufs, which):
        bufs[group] = src[...]
        for k in range(1, 2 * NX):
            send(
                src, bufs.at[group],
                row_send_sem.at[which, k - 1], row_recv_sem.at[which, group], at_group(k),
            )
        for k in range(1, 2 * NX):
            other = lax.rem(group + k, 2 * NX)
            arrived(bufs.at[other], row_recv_sem.at[which, other])

    def exchange_y(src, bufs, which):
        bufs[y] = src[...]
        for k in range(1, NY):
            send(
                src, bufs.at[y],
                y_send_sem.at[which, k - 1], y_recv_sem.at[which, y], at_y(k),
            )
        for k in range(1, NY):
            other = lax.rem(y + k, NY)
            arrived(bufs.at[other], y_recv_sem.at[which, other])

    def exchange_z(src, bufs, which):
        bufs[z] = src[...]
        for k in range(1, NZ):
            send(
                src, bufs.at[z],
                col_send_sem.at[which, k - 1], col_recv_sem.at[which, z], at_z(k),
            )
        for k in range(1, NZ):
            other = lax.rem(z + k, NZ)
            arrived(bufs.at[other], col_recv_sem.at[which, other])

    def merged(bufs, n):
        highest = bufs[0, 0:1, :]
        for k in range(1, n):
            highest = jnp.maximum(highest, bufs[k, 0:1, :])
        total = jnp.zeros_like(highest)
        for k in range(n):
            total = total + bufs[k, 1:2, :] * jnp.exp(bufs[k, 0:1, :] - highest)
        return highest, total

    def added(bufs, n):
        total = bufs[0]
        for k in range(1, n):
            total = total + bufs[k]
        return total

    def to_lanes(part):
        return jnp.transpose(part)

    def to_columns(vec):
        return jnp.transpose(jnp.broadcast_to(vec, (BLK, COLS)))

    exchange_group(row_vec, row_buf0, 0)
    highest, total = merged(row_buf0, 2 * NX)
    y_vec[0:1, :] = highest
    y_vec[1:2, :] = total
    exchange_y(y_vec, y_buf0, 0)
    highest, total = merged(y_buf0, NY)
    pot[...] = -(highest + jnp.log(total))

    def column_stats(g, carry):
        rows = pl.ds(pl.multiple_of(g * 8, 8), 8)
        tiles = [
            logits[rows, k * BLK:(k + 1) * BLK] + pot[:, k * BLK:(k + 1) * BLK] for k in range(SLOTS)
        ]
        highest = tiles[0]
        for tile in tiles[1:]:
            highest = jnp.maximum(highest, tile)
        total = jnp.exp(tiles[0] - highest)
        for tile in tiles[1:]:
            total = total + jnp.exp(tile - highest)
        col_part[rows, :] = highest
        col_part2[rows, :] = total
        return carry

    lax.fori_loop(0, COLS // 8, column_stats, 0)
    peaks = to_lanes(col_part[...])
    sums = to_lanes(col_part2[...])
    highest = jnp.max(peaks, axis=0, keepdims=True)
    col_send0[0:1, :] = highest
    col_send0[1:2, :] = jnp.sum(sums * jnp.exp(peaks - highest), axis=0, keepdims=True)
    exchange_z(col_send0, col_buf0, 0)
    highest, total = merged(col_buf0, NZ)
    col_vec[...] = to_columns(BALANCE - (highest + jnp.log(total)))

    WIDE = 2 * BLK

    def first_rows(t, carry):
        lanes = pl.ds(pl.multiple_of(t * WIDE, WIDE), WIDE)
        col = col_vec[...]
        both = jnp.concatenate([col, col], axis=1)
        plan = jnp.exp(logits[:, lanes] + pot[:, lanes] + both)
        logits[:, lanes] = plan
        row_sums[:, lanes] = jnp.sum(plan, axis=0, keepdims=True)
        return carry

    def later_rows(t, carry):
        lanes = pl.ds(pl.multiple_of(t * WIDE, WIDE), WIDE)
        col = col_vec[...]
        both = jnp.concatenate([col, col], axis=1)
        row_sums[:, lanes] = jnp.sum(logits[:, lanes] * both, axis=0, keepdims=True)
        return carry

    def row_factor(which):
        row_vec1 = row_buf.at[which - 1]
        y_bufs = y_buf.at[which - 1]
        src = row_src.at[which - 1]
        src[...] = row_sums[...]
        exchange_group(src, row_vec1, which)
        mid = y_src.at[which - 1]
        mid[...] = added(row_vec1, 2 * NX)
        exchange_y(mid, y_bufs, which)
        pot[...] = 1.0 / added(y_bufs, NY)

    row_src = row_buf.at[:, 2 * NX]
    y_src = y_buf.at[:, NY]

    def column_sums(g, carry):
        rows = pl.ds(pl.multiple_of(g * 32, 32), 32)
        total = logits[rows, 0:BLK] * pot[:, 0:BLK]
        for k in range(1, SLOTS):
            total = total + logits[rows, k * BLK:(k + 1) * BLK] * pot[:, k * BLK:(k + 1) * BLK]
        col_part[rows, :] = total
        return carry

    def column_total(which):
        src = col_send.at[which - 1]
        src[...] = jnp.sum(to_lanes(col_part[...]), axis=0, keepdims=True)
        bufs = col_buf.at[which - 1]
        exchange_z(src, bufs, which)
        return added(bufs, NZ)

    lax.fori_loop(0, NR // WIDE, first_rows, 0)
    row_factor(1)
    for sweep in (1, 2):
        lax.fori_loop(0, COLS // 32, column_sums, 0)
        col_vec[...] = to_columns((ROWS / KB) / column_total(sweep))
        lax.fori_loop(0, NR // WIDE, later_rows, 0)
        row_factor(sweep + 1)

    def make_transport(g, carry):
        rows = pl.ds(pl.multiple_of(g * 32, 32), 32)
        col = col_vec[rows, :]
        mass = jnp.zeros((32, BLK), jnp.float32)
        for k in range(SLOTS):
            lanes = slice(k * BLK, (k + 1) * BLK)
            rounded = (logits[rows, lanes] * pot[:, lanes] * col).astype(jnp.bfloat16)
            transport[rows, lanes] = rounded
            mass = mass + rounded.astype(jnp.float32)
        col_part[rows, :] = mass
        return carry

    lax.fori_loop(0, COLS // 32, make_transport, 0)

    def weigh(d0, d1):
        def rows_of(d):
            return transport[pl.ds(pl.multiple_of(lax.rem(z + d + NZ, NZ) * OWN, OWN), OWN), :]

        left = jnp.concatenate([rows_of(d0), rows_of(d1)], axis=0)

        def body(n, carry):
            lanes = pl.ds(pl.multiple_of(n * 256, 256), 256)
            both = jnp.dot(left, emb[:, lanes], preferred_element_type=jnp.float32)
            partial[d0 % NZ, :, lanes] = both[:OWN]
            partial[d1 % NZ, :, lanes] = both[OWN:]
            return carry

        lax.fori_loop(0, E // 256, body, 0)

    def features(h):
        return slice(h * HALF, (h + 1) * HALF)

    def long_step(h, s):
        way = 1 - 2 * h
        value = partial[(way * (4 - s)) % NZ, :, features(h)]
        if s:
            arrived(long_in.at[h * 4 + s - 1], long_recv_sem.at[h * 4 + s - 1])
            value = value + long_in[h * 4 + s - 1].astype(jnp.float32)
        at = h * 4 + s
        long_out[at] = value.astype(SUM_TYPE)
        send(long_out.at[at], long_in.at[at], long_send_sem.at[at], long_recv_sem.at[at], at_z(way))

    def short_step(h, s):
        way = 2 * h - 1
        value = partial[(way * (3 - s)) % NZ, :, features(h)]
        if s:
            arrived(short_in.at[h * 3 + s - 1], short_recv_sem.at[h * 3 + s - 1])
            value = value + short_in[h * 3 + s - 1].astype(jnp.float32)
        at = h * 3 + s
        short_out[at] = value.astype(SUM_TYPE)
        send(short_out.at[at], short_in.at[at], short_send_sem.at[at], short_recv_sem.at[at], at_z(way))

    weigh(4, 3)
    long_step(0, 0)
    long_step(1, 0)
    short_step(1, 0)
    weigh(-3, 2)
    short_step(0, 0)
    weigh(-2, 1)
    long_step(0, 1)
    long_step(1, 1)
    short_step(0, 1)
    short_step(1, 1)
    weigh(-1, 0)
    col_vec[...] = to_columns(column_total(3))
    long_step(0, 2)
    long_step(1, 2)
    short_step(0, 2)
    short_step(1, 2)
    long_step(0, 3)
    long_step(1, 3)
    mass = col_vec[pl.ds(pl.multiple_of(z * OWN, OWN), OWN), :][:, :1]
    for h in (0, 1):
        arrived(short_in.at[h * 3 + 2], short_recv_sem.at[h * 3 + 2])
        weighted = partial[0, :, features(h)] + short_in[h * 3 + 2].astype(jnp.float32)
        arrived(long_in.at[h * 4 + 3], long_recv_sem.at[h * 4 + 3])
        weighted = weighted + long_in[h * 4 + 3].astype(jnp.float32)
        grad[:, features(h)] = (mass * cent[:, features(h)] - weighted) * (KB / ROWS)

    for copy in pending:
        copy.wait_send()


def per_device(stream, sample_index, centroids, first_moment, second_moment):
    f32 = jnp.float32
    scratch = [
        pltpu.VMEM((NR, E), jnp.bfloat16),
        pltpu.VMEM((COLS, E), jnp.bfloat16),
        pltpu.VMEM((COLS, NR), f32),
        pltpu.VMEM((COLS, NR), jnp.bfloat16),
        pltpu.VMEM((COLS, BLK), f32),
        pltpu.VMEM((COLS, BLK), f32),
        pltpu.VMEM((COLS, BLK), f32),
        pltpu.VMEM((COLS, BLK), f32),
        pltpu.VMEM((2, NR), f32),
        pltpu.VMEM((2 * NX, 2, NR), f32),
        pltpu.VMEM((3, 2 * NX + 1, 1, NR), f32),
        pltpu.VMEM((1, NR), f32),
        pltpu.VMEM((2, NR), f32),
        pltpu.VMEM((NY, 2, NR), f32),
        pltpu.VMEM((3, NY + 1, 1, NR), f32),
        pltpu.VMEM((1, NR), f32),
        pltpu.VMEM((2, COLS), f32),
        pltpu.VMEM((3, 1, COLS), f32),
        pltpu.VMEM((NZ, 2, COLS), f32),
        pltpu.VMEM((3, NZ, 1, COLS), f32),
        pltpu.VMEM((NZ, OWN, E), f32),
        pltpu.VMEM((8, OWN, HALF), SUM_TYPE),
        pltpu.VMEM((6, OWN, HALF), SUM_TYPE),
        pltpu.VMEM((8, OWN, HALF), SUM_TYPE),
        pltpu.VMEM((6, OWN, HALF), SUM_TYPE),
        pltpu.SemaphoreType.DMA((24,)),
        pltpu.SemaphoreType.DMA((SLOTS,)),
        pltpu.SemaphoreType.DMA,
        pltpu.SemaphoreType.DMA,
        pltpu.SemaphoreType.DMA((7,)),
        pltpu.SemaphoreType.DMA((NZ,)),
        pltpu.SemaphoreType.DMA((4, 2 * NX - 1)),
        pltpu.SemaphoreType.DMA((4, 2 * NX)),
        pltpu.SemaphoreType.DMA((4, NY - 1)),
        pltpu.SemaphoreType.DMA((4, NY)),
        pltpu.SemaphoreType.DMA((4, NZ - 1)),
        pltpu.SemaphoreType.DMA((4, NZ)),
        pltpu.SemaphoreType.DMA((8,)),
        pltpu.SemaphoreType.DMA((8,)),
        pltpu.SemaphoreType.DMA((6,)),
        pltpu.SemaphoreType.DMA((6,)),
    ]
    gradient = pl.pallas_call(
        kernel,
        out_shape=jax.ShapeDtypeStruct((OWN, E), f32),
        in_specs=[pl.BlockSpec(memory_space=pltpu.VMEM)] * 3,
        out_specs=pl.BlockSpec(memory_space=pltpu.VMEM),
        scratch_shapes=scratch,
        compiler_params=pltpu.CompilerParams(
            collective_id=0, has_side_effects=True, vmem_limit_bytes=56 * 1024 * 1024
        ),
        cost_estimate=pl.CostEstimate(
            flops=4 * NR * COLS * E, bytes_accessed=4 * 1024 * 1024, transcendentals=3 * NR * COLS
        ),
        name="balanced_kmeans",
    )(stream, sample_index.reshape(ND // BLK, BLK), centroids)
    new_first = beta_one * first_moment + (1.0 - beta_one) * gradient
    new_second = beta_two * second_moment + (1.0 - beta_two) * gradient * gradient
    new_centroids = centroids - step_rate * new_first / (jnp.sqrt(new_second) + epsilon)
    return (new_centroids, new_first, new_second)


def solution(mesh):
    cut = P(("cent", "dp"), None)
    return jax.shard_map(
        per_device,
        mesh=mesh,
        in_specs=(P("dp", None), P("dp"), cut, cut, cut),
        out_specs=(cut, cut, cut),
        check_vma=False,
    )
```

time: 890 us -> 129 us (0.14)
  blocking collectives: 594 us -> 0 us
  waiting for transfers between devices: 189 us -> 0 us
  Pallas kernels: 0 us -> 126 us
  other arithmetic: 66.1 us -> 1.79 us
  matrix products: 19.4 us -> 0 us
  between operations: 14.3 us -> 0.69 us
    psum x8 -> x0, blocking collectives: 334 us -> none  [the longest x3 210 us: per_device(): lax.psum(column_summed * jnp.exp(column_highest - column_overall), 'dp')]
    pmax x7 -> x0, blocking collectives: 259 us -> none  [the longest x3 209 us: per_device(): column_overall = lax.pmax(column_highest, 'dp')]
    pallas_call x0 -> x1, Pallas kernels: none -> 126 us  [per_device(): pl.pallas_call(kernel, out_shape=jax.ShapeDtypeStruct((OWN, E), f32), in_...]
    psum x1 -> x0, waiting for transfers between devices: 111 us -> none  [per_device(): weighted, weight_mass = lax.psum((weighted, weight_mass), 'dp')]
    all_gather x1 -> x0, waiting for transfers between devices: 77.8 us -> none  [per_device(): shard_piece = lax.all_gather(rounded, 'dp', axis=0, tiled=True)]
    reduce_sum x9 -> x0, other arithmetic: 37.5 us -> none  [the longest x4 17.7 us: row_potential(): summed = jnp.sum(jnp.exp(shifted - highest[:, None]), axis=1)]
    reduce_max x6 -> x0, other arithmetic: 24.1 us -> none  [the longest x3 12.1 us: row_potential(): highest = jnp.max(shifted, axis=1)]
    dot_general x2 -> x0, matrix products: 19.4 us -> none  [the longest x1 10.4 us: per_device(): lax.dot_general(transport, embedded, (((0,), (0,)), ((), ())), preferred_...]
  transfers between devices with their start and end apart: 2 -> 0, of which waited for: 2 -> 0; matrix products, arithmetic and copies ran while one was open for 1% -> 0% of each run, Pallas kernels for 0% -> 0%
where the time goes in v1:
time: 129 us
  Pallas kernels  126 us (98%)
  other arithmetic  1.79 us (1%)
    pallas_call x1, Pallas kernels, per_device(): pl.pallas_call(kernel, out_shape=jax.ShapeDtypeStruct((OWN, E), f32), in_...  126 us

profile of v1, /device:TPU:8, one launch (start us, length us, event | category | flops | bytes accessed | tf_op | source)
XLA Modules:
  0.0 128.6 jit_solution(14146822838271484765)
XLA Ops:
  0.6 0.0 copy-start
  0.6 0.0 copy-start.1
  0.7 0.0 copy-start.2
  0.7 126.1 %balanced_kmeans.1 = f32[64,768]{1,0:T(8,128)} custom-call(bf16[2048,768]{1,0:T(8,128)(2,1)} %stream.1, s32[8,128]{1,0:T(8,128)} %bitcast.1, f32[64,768]{1,0:T(8,128)} %cent.1), custom_call_target="tpu_custom_call" | custom-call | flops 6442450944 | bytes 4194304 | tf_op jit(solution)/shard_map/balanced_kmeans/pallas_call | solution.py:495
  126.8 0.0 copy-done
  126.8 0.0 copy-done.1
  126.8 0.0 copy-done.2
  126.8 1.8 %divide_subtract_fusion = (f32[64,768]{1,0:T(8,128)}, f32[64,768]{1,0:T(8,128)}, f32[64,768]{1,0:T(8,128)}) fusion(f32[64,768]{1,0:T(8,128)S(1)} %copy-done, f32[64,768]{1,0:T(8,128)} %balanced_kmeans.1, f32[64,768]{1,0:T(8,128)S(1)} %copy-done.1, f32[64,768]{1,0:T(8,128)S(1)} %copy-done.2), kind=kLoop, calls=%fused_computation.2 | loop fusion | flops 540672 | bytes 1376256 | tf_op jit(solution)/shard_map/sub | solution.py:511
Async XLA Ops:
  0.6 126.2 %copy-start = (f32[64,768]{1,0:T(8,128)S(1)}, f32[64,768]{1,0:T(8,128)}, u32[]{:S(2)}) copy-start(f32[64,768]{1,0:T(8,128)} %cent.1) | copy-start | bytes 589828
  0.6 126.2 %copy-start.1 = (f32[64,768]{1,0:T(8,128)S(1)}, f32[64,768]{1,0:T(8,128)}, u32[]{:S(2)}) copy-start(f32[64,768]{1,0:T(8,128)} %param.8) | copy-start | bytes 589828
  0.7 126.2 %copy-start.2 = (f32[64,768]{1,0:T(8,128)S(1)}, f32[64,768]{1,0:T(8,128)}, u32[]{:S(2)}) copy-start(f32[64,768]{1,0:T(8,128)} %param.9) | copy-start | bytes 589828

commit v2 on v1

--- a/solution.py
+++ b/solution.py
@@ -22,7 +22,7 @@
 NR = SLOTS * BLK
 STREAM = 2 * ND
 BALANCE = math.log(ROWS / KB)
-SUM_TYPE = jnp.float32
+SUM_TYPE = jnp.bfloat16
 HALF = E // 2
 
 beta_one = 0.9
@@ -31,22 +31,15 @@
 epsilon = 1e-08
 
 
-def pick(i, values):
-    chosen = values[0]
-    for k, value in enumerate(values[1:], 1):
-        chosen = jnp.where(i == k, value, chosen)
-    return chosen
-
-
 def kernel(
-    stream, idx, cent, grad,
-    emb, piece, logits, transport, half_sq, col_part, col_part2, col_vec,
+    stream_hbm, idx, cent, grad,
+    stream,    emb, piece, logits, transport, half_sq, col_part, col_part2, col_vec,
     row_vec, row_buf0, row_buf, row_sums, y_vec, y_buf0, y_buf, pot,
     col_send0, col_send, col_buf0, col_buf,
     partial, long_out, short_out, long_in, short_in,
     emb_send, emb_recv, sib_send, sib_recv, z_send, z_recv,
     row_send_sem, row_recv_sem, y_send_sem, y_recv_sem, col_send_sem, col_recv_sem,
-    long_send_sem, long_recv_sem, short_send_sem, short_recv_sem,
+    long_send_sem, long_recv_sem, short_send_sem, short_recv_sem, load_sem,
 ):
     dp = lax.axis_index("dp")
     group = lax.axis_index("cent")
@@ -68,12 +61,10 @@
     sibling = {"dp": dp, "cent": x * 2 + 1 - core}
 
     barrier = pltpu.get_barrier_semaphore()
-    for k in range(1, 2 * NX):
-        pl.semaphore_signal(barrier, inc=1, device_id=at_group(k), device_id_type=MESH)
-    for k in range(1, NY):
-        pl.semaphore_signal(barrier, inc=1, device_id=at_y(k), device_id_type=MESH)
-    for k in range(1, NZ):
-        pl.semaphore_signal(barrier, inc=1, device_id=at_z(k), device_id_type=MESH)
+    for device in (sibling, at_x(1), at_x(-1), at_y(1), at_y(-1), at_z(1), at_z(-1)):
+        pl.semaphore_signal(barrier, inc=1, device_id=device, device_id_type=MESH)
+    load = pltpu.make_async_copy(stream_hbm, stream, load_sem)
+    load.start()
 
     pending = []
 
@@ -100,24 +91,35 @@
     sends = [0]
 
     def send_block(slot, device):
-        send(emb_at(slot), emb_at(slot), emb_send.at[sends[0]], emb_recv.at[slot], device)
+        send(emb_at(slot), emb_at(slot), emb_send.at[sends[0]], emb_recv.at[slot, 0], device)
         sends[0] += 1
 
     def wait_block(slot):
-        arrived(emb_at(slot), emb_recv.at[slot])
-
-    def piece_at(k):
-        return piece.at[pl.ds(pl.multiple_of(lax.rem(z + k + NZ, NZ) * OWN, OWN), OWN), :]
+        arrived(emb_at(slot), emb_recv.at[slot, 0])
+
+    def half_at(slot, h):
+        return emb.at[pl.ds(pl.multiple_of(slot * BLK + h * (BLK // 2), BLK // 2), BLK // 2), :]
+
+    def send_half(slot, h, device):
+        send(half_at(slot, h), half_at(slot, h), emb_send.at[sends[0]], emb_recv.at[slot, h], device)
+        sends[0] += 1
+
+    def piece_at(k, h):
+        owner = lax.rem(z + k + NZ, NZ)
+        return piece.at[pl.ds(pl.multiple_of(owner * OWN + h * (OWN // 2), OWN // 2), OWN // 2), :]
 
     z_sends = [0]
 
-    def send_piece(k, toward):
+    def send_piece(k, h, toward):
         owner = lax.rem(z + k + NZ, NZ)
-        send(piece_at(k), piece_at(k), z_send.at[z_sends[0]], z_recv.at[owner], at_z(toward))
+        send(piece_at(k, h), piece_at(k, h), z_send.at[z_sends[0]], z_recv.at[owner, h], at_z(toward))
         z_sends[0] += 1
 
-    def wait_piece(k):
-        arrived(piece_at(k), z_recv.at[lax.rem(z + k + NZ, NZ)])
+    def on_pieces(k, h, forward=True):
+        for d in (-k, k):
+            arrived(piece_at(d, h), z_recv.at[lax.rem(z + d + NZ, NZ), h])
+            if forward or (d == -3):
+                send_piece(d, h, 1 if d < 0 else -1)
 
     def gather(j):
         quarter = lax.rem(x + j, 4)
@@ -131,96 +133,107 @@
         return slot
 
     piece[pl.ds(pl.multiple_of(z * OWN, OWN), OWN), :] = cent[...].astype(jnp.bfloat16)
+    load.wait()
     first = gather(0)
-    pl.semaphore_wait(barrier, 2 * NX + NY + NZ - 3)
-    send_block(first, at_y(1))
-    send_block(first, at_y(-1))
-    send_piece(0, 1)
-    send_piece(0, -1)
+    pl.semaphore_wait(barrier, 7)
+    for h in (0, 1):
+        send_piece(0, h, 1)
+        send_piece(0, h, -1)
+        send_half(first, h, at_y(1))
+        send_half(first, h, at_y(-1))
     second = gather(2)
-    send_block(second, at_y(1))
-    send_block(second, at_y(-1))
     gather(1)
     gather(3)
     own_first = y * 8 + core * 4
     send(emb_at(own_first, 4), emb_at(own_first, 4), sib_send, sib_recv, sibling)
 
-    def on_piece(k, forward):
-        wait_piece(k)
+    def on_half(k, j, h, forward=False, spread=False):
+        slot = slot_of(k, core, j)
+        arrived(half_at(slot, h), emb_recv.at[slot, h])
         if forward:
-            send_piece(k, 1 if k < 0 else -1)
-
-    def on_block(k, j, forward=(), spread=False):
+            send_half(slot, h, at_y(1))
+        if spread:
+            send_half(slot, h, at_x(1))
+            send_half(slot, h, at_x(-1))
+        if h:
+            send_block(slot, sibling)
+
+    def on_block(k, j, forward=False):
         slot = slot_of(k, core, j)
         wait_block(slot)
-        for toward in forward:
-            send_block(slot, at_y(toward))
-        if spread:
-            send_block(slot, at_x(1))
-            send_block(slot, at_x(-1))
+        if forward:
+            send_block(slot, at_y(-1))
         send_block(slot, sibling)
 
-    def score(slot):
-        lanes = pl.ds(pl.multiple_of(slot * BLK, BLK), BLK)
-        rows = emb[pl.ds(pl.multiple_of(slot * BLK, BLK), BLK), :]
+    def score(blocks):
+        starts = [pl.multiple_of(slot * BLK, BLK) for slot in blocks]
+        rows = jnp.concatenate([emb[pl.ds(start, BLK), :] for start in starts], axis=0)
         product = lax.dot_general(
             piece[...], rows, (((1,), (1,)), ((), ())), preferred_element_type=jnp.float32
         )
-        values = product - half_sq[...]
-        logits[:, lanes] = values
-        highest = jnp.max(values, axis=0, keepdims=True)
-        row_vec[0:1, lanes] = highest
-        row_vec[1:2, lanes] = jnp.sum(jnp.exp(values - highest), axis=0, keepdims=True)
-
-    def score_all(offsets, c, wait):
-        slots = [slot_of(k, c, j) for k, j in offsets]
-
-        def body(i, carry):
-            slot = pick(i, slots)
-            if wait:
+        less = half_sq[...]
+        for k, start in enumerate(starts):
+            lanes = pl.ds(start, BLK)
+            values = product[:, k * BLK:(k + 1) * BLK] - less
+            logits[:, lanes] = values
+            highest = jnp.max(values, axis=0, keepdims=True)
+            row_vec[0:1, lanes] = highest
+            row_vec[1:2, lanes] = jnp.sum(jnp.exp(values - highest), axis=0, keepdims=True)
+
+    def score_from(offsets, c):
+        blocks = [slot_of(k, c, j) for k, j in offsets]
+        if offsets[0][0] and c is not core:
+            for slot in blocks:
                 wait_block(slot)
-            score(slot)
-            return carry
-
-        lax.fori_loop(0, len(slots), body, 0)
-
-    wave1 = [(-1, 0), (1, 0)]
-    wave2 = [(2, 0), (-1, 1), (-1, 3), (1, 2)]
-    wave3 = [(1, 1), (1, 3), (-1, 2), (2, 2)]
-    wave4 = [(2, 1), (2, 3)]
-
-    on_piece(-1, True)
-    on_piece(1, True)
-    on_block(-1, 0, forward=(1,), spread=True)
-    on_block(1, 0, spread=True)
-    on_piece(-2, True)
-    on_piece(2, True)
-    on_piece(-3, True)
-    on_piece(3, False)
-    on_block(2, 0, spread=True)
-    on_block(1, 2, forward=(-1,))
-    on_block(-1, 1)
-    on_block(-1, 3)
-    on_piece(-4, False)
+        score(blocks)
+
+    own = [(0, 0), (0, 1), (0, 2), (0, 3)]
+    early = [(-1, 0), (1, 0), (2, 0), (1, 2)]
+    middle = [(-1, 1), (-1, 3), (1, 1), (1, 3)]
+    late = [(-1, 2), (2, 2), (2, 1), (2, 3)]
+    other = 1 - core
+
+    on_pieces(1, 0)
+    on_half(-1, 0, 0, forward=True, spread=True)
+    on_half(1, 0, 0, spread=True)
+    on_pieces(1, 1)
+    on_half(-1, 0, 1, forward=True, spread=True)
+    on_half(1, 0, 1, spread=True)
+    send_block(second, at_y(1))
+    send_block(second, at_y(-1))
+    on_pieces(2, 0)
+    on_pieces(2, 1)
+    on_half(2, 0, 0, spread=True)
+    on_pieces(3, 0, False)
+    on_half(2, 0, 1, spread=True)
+    on_pieces(3, 1, False)
+    on_block(1, 2, forward=True)
+    for h in (0, 1):
+        on_half(-1, 1, h)
+        on_half(-1, 3, h)
+    for h in (0, 1):
+        arrived(piece_at(-4, h), z_recv.at[lax.rem(z + 4, NZ), h])
     whole = piece[...].astype(jnp.float32)
     half_sq[...] = jnp.broadcast_to(
         0.5 * jnp.sum(whole * whole, axis=1, keepdims=True), (COLS, BLK)
     )
-    score_all([(0, 0), (0, 1), (0, 2), (0, 3)], core, False)
-    score_all(wave1, core, False)
-    arrived(emb_at(y * 8 + (1 - core) * 4, 4), sib_recv)
-    score_all([(0, 0), (0, 1), (0, 2), (0, 3)], 1 - core, False)
-    score_all(wave1, 1 - core, True)
-    score_all(wave2, core, False)
-    for k, j in wave3:
-        on_block(k, j)
-    score_all(wave2, 1 - core, True)
-    score_all(wave3, core, False)
-    for k, j in wave4:
-        on_block(k, j)
-    score_all(wave3, 1 - core, True)
-    score_all(wave4, core, False)
-    score_all(wave4, 1 - core, True)
+    score_from(own, core)
+    score_from(early, core)
+    arrived(emb_at(y * 8 + other * 4, 4), sib_recv)
+    score_from(own, other)
+    for h in (0, 1):
+        on_half(1, 1, h)
+        on_half(1, 3, h)
+    on_block(-1, 2)
+    score_from(early, other)
+    score_from(middle, core)
+    on_block(2, 2)
+    for h in (0, 1):
+        on_half(2, 1, h)
+        on_half(2, 3, h)
+    score_from(middle, other)
+    score_from(late, core)
+    score_from(late, other)
 
     def exchange_group(src, bufs, which):
         bufs[group] = src[...]
@@ -244,16 +257,22 @@
             other = lax.rem(y + k, NY)
             arrived(bufs.at[other], y_recv_sem.at[which, other])
 
-    def exchange_z(src, bufs, which):
-        bufs[z] = src[...]
+    def start_z(src, bufs, which):
         for k in range(1, NZ):
             send(
                 src, bufs.at[z],
                 col_send_sem.at[which, k - 1], col_recv_sem.at[which, z], at_z(k),
             )
+        bufs[z] = src[...]
+
+    def finish_z(bufs, which):
         for k in range(1, NZ):
             other = lax.rem(z + k, NZ)
             arrived(bufs.at[other], col_recv_sem.at[which, other])
+
+    def exchange_z(src, bufs, which):
+        start_z(src, bufs, which)
+        finish_z(bufs, which)
 
     def merged(bufs, n):
         highest = bufs[0, 0:1, :]
@@ -285,7 +304,7 @@
     pot[...] = -(highest + jnp.log(total))
 
     def column_stats(g, carry):
-        rows = pl.ds(pl.multiple_of(g * 8, 8), 8)
+        rows = pl.ds(pl.multiple_of(g * 16, 16), 16)
         tiles = [
             logits[rows, k * BLK:(k + 1) * BLK] + pot[:, k * BLK:(k + 1) * BLK] for k in range(SLOTS)
         ]
@@ -299,7 +318,7 @@
         col_part2[rows, :] = total
         return carry
 
-    lax.fori_loop(0, COLS // 8, column_stats, 0)
+    lax.fori_loop(0, COLS // 16, column_stats, 0)
     peaks = to_lanes(col_part[...])
     sums = to_lanes(col_part2[...])
     highest = jnp.max(peaks, axis=0, keepdims=True)
@@ -349,18 +368,21 @@
         col_part[rows, :] = total
         return carry
 
-    def column_total(which):
+    def start_total(which):
         src = col_send.at[which - 1]
         src[...] = jnp.sum(to_lanes(col_part[...]), axis=0, keepdims=True)
-        bufs = col_buf.at[which - 1]
-        exchange_z(src, bufs, which)
-        return added(bufs, NZ)
+        start_z(src, col_buf.at[which - 1], which)
+
+    def finish_total(which):
+        finish_z(col_buf.at[which - 1], which)
+        return added(col_buf.at[which - 1], NZ)
 
     lax.fori_loop(0, NR // WIDE, first_rows, 0)
     row_factor(1)
     for sweep in (1, 2):
         lax.fori_loop(0, COLS // 32, column_sums, 0)
-        col_vec[...] = to_columns((ROWS / KB) / column_total(sweep))
+        start_total(sweep)
+        col_vec[...] = to_columns((ROWS / KB) / finish_total(sweep))
         lax.fori_loop(0, NR // WIDE, later_rows, 0)
         row_factor(sweep + 1)
 
@@ -416,6 +438,7 @@
         short_out[at] = value.astype(SUM_TYPE)
         send(short_out.at[at], short_in.at[at], short_send_sem.at[at], short_recv_sem.at[at], at_z(way))
 
+    start_total(3)
     weigh(4, 3)
     long_step(0, 0)
     long_step(1, 0)
@@ -428,13 +451,13 @@
     short_step(0, 1)
     short_step(1, 1)
     weigh(-1, 0)
-    col_vec[...] = to_columns(column_total(3))
     long_step(0, 2)
     long_step(1, 2)
     short_step(0, 2)
     short_step(1, 2)
     long_step(0, 3)
     long_step(1, 3)
+    col_vec[...] = to_columns(finish_total(3))
     mass = col_vec[pl.ds(pl.multiple_of(z * OWN, OWN), OWN), :][:, :1]
     for h in (0, 1):
         arrived(short_in.at[h * 3 + 2], short_recv_sem.at[h * 3 + 2])
@@ -450,6 +473,7 @@
 def per_device(stream, sample_index, centroids, first_moment, second_moment):
     f32 = jnp.float32
     scratch = [
+        pltpu.VMEM((STREAM, E), jnp.bfloat16),
         pltpu.VMEM((NR, E), jnp.bfloat16),
         pltpu.VMEM((COLS, E), jnp.bfloat16),
         pltpu.VMEM((COLS, NR), f32),
@@ -475,12 +499,12 @@
         pltpu.VMEM((6, OWN, HALF), SUM_TYPE),
         pltpu.VMEM((8, OWN, HALF), SUM_TYPE),
         pltpu.VMEM((6, OWN, HALF), SUM_TYPE),
-        pltpu.SemaphoreType.DMA((24,)),
-        pltpu.SemaphoreType.DMA((SLOTS,)),
+        pltpu.SemaphoreType.DMA((40,)),
+        pltpu.SemaphoreType.DMA((SLOTS, 2)),
         pltpu.SemaphoreType.DMA,
         pltpu.SemaphoreType.DMA,
-        pltpu.SemaphoreType.DMA((7,)),
-        pltpu.SemaphoreType.DMA((NZ,)),
+        pltpu.SemaphoreType.DMA((14,)),
+        pltpu.SemaphoreType.DMA((NZ, 2)),
         pltpu.SemaphoreType.DMA((4, 2 * NX - 1)),
         pltpu.SemaphoreType.DMA((4, 2 * NX)),
         pltpu.SemaphoreType.DMA((4, NY - 1)),
@@ -491,11 +515,12 @@
         pltpu.SemaphoreType.DMA((8,)),
         pltpu.SemaphoreType.DMA((6,)),
         pltpu.SemaphoreType.DMA((6,)),
+        pltpu.SemaphoreType.DMA,
     ]
     gradient = pl.pallas_call(
         kernel,
         out_shape=jax.ShapeDtypeStruct((OWN, E), f32),
-        in_specs=[pl.BlockSpec(memory_space=pltpu.VMEM)] * 3,
+        in_specs=[pl.BlockSpec(memory_space=pl.ANY)] + [pl.BlockSpec(memory_space=pltpu.VMEM)] * 2,
         out_specs=pl.BlockSpec(memory_space=pltpu.VMEM),
         scratch_shapes=scratch,
         compiler_params=pltpu.CompilerParams(

time: 129 us -> 112 us (0.87)
  Pallas kernels: 126 us -> 109 us
    pallas_call x1, Pallas kernels: 126 us -> 109 us  [per_device(): pl.pallas_call(kernel, out_shape=jax.ShapeDtypeStruct((OWN, E), f32), in_...]
where the time goes in v2:
time: 112 us; the launch traced here: 111 us
  Pallas kernels  109 us (97%)
  other arithmetic  1.79 us (2%)
    pallas_call x1, Pallas kernels, per_device(): pl.pallas_call(kernel, out_shape=jax.ShapeDtypeStruct((OWN, E), f32), in_...  109 us

profile of v2, /device:TPU:8, one launch (start us, length us, event | category | flops | bytes accessed | tf_op | source)
XLA Modules:
  0.0 111.2 jit_solution(7477112985775746482)
XLA Ops:
  0.6 0.0 copy-start
  0.6 0.0 copy-start.1
  0.7 0.0 copy-start.2
  0.7 108.7 %balanced_kmeans.1 = f32[64,768]{1,0:T(8,128)} custom-call(bf16[2048,768]{1,0:T(8,128)(2,1)} %stream_hbm.1, s32[8,128]{1,0:T(8,128)} %bitcast.1, f32[64,768]{1,0:T(8,128)} %cent.1), custom_call_target="tpu_custom_call" | custom-call | flops 6442450944 | bytes 4194304 | tf_op jit(solution)/shard_map/balanced_kmeans/pallas_call | solution.py:520
  109.4 0.0 copy-done
  109.4 0.0 copy-done.1
  109.4 0.0 copy-done.2
  109.4 1.8 %divide_subtract_fusion = (f32[64,768]{1,0:T(8,128)}, f32[64,768]{1,0:T(8,128)}, f32[64,768]{1,0:T(8,128)}) fusion(f32[64,768]{1,0:T(8,128)S(1)} %copy-done, f32[64,768]{1,0:T(8,128)} %balanced_kmeans.1, f32[64,768]{1,0:T(8,128)S(1)} %copy-done.1, f32[64,768]{1,0:T(8,128)S(1)} %copy-done.2), kind=kLoop, calls=%fused_computation.2 | loop fusion | flops 540672 | bytes 1376256 | tf_op jit(solution)/shard_map/sub | solution.py:536
Async XLA Ops:
  0.6 108.7 %copy-start = (f32[64,768]{1,0:T(8,128)S(1)}, f32[64,768]{1,0:T(8,128)}, u32[]{:S(2)}) copy-start(f32[64,768]{1,0:T(8,128)} %cent.1) | copy-start | bytes 589828
  0.6 108.7 %copy-start.1 = (f32[64,768]{1,0:T(8,128)S(1)}, f32[64,768]{1,0:T(8,128)}, u32[]{:S(2)}) copy-start(f32[64,768]{1,0:T(8,128)} %param.8) | copy-start | bytes 589828
  0.7 108.7 %copy-start.2 = (f32[64,768]{1,0:T(8,128)S(1)}, f32[64,768]{1,0:T(8,128)}, u32[]{:S(2)}) copy-start(f32[64,768]{1,0:T(8,128)} %param.9) | copy-start | bytes 589828

commit v3 on v2

--- a/solution.py
+++ b/solution.py
@@ -23,7 +23,9 @@
 STREAM = 2 * ND
 BALANCE = math.log(ROWS / KB)
 SUM_TYPE = jnp.bfloat16
-HALF = E // 2
+CHUNK = 384
+CHUNKS = E // CHUNK
+PLANE = NX * NY
 
 beta_one = 0.9
 beta_two = 0.99
@@ -31,14 +33,20 @@
 epsilon = 1e-08
 
 
+def halving(op, parts):
+    while len(parts) > 1:
+        parts = [op(a, b) for a, b in zip(parts[::2], parts[1::2])]
+    return parts[0]
+
+
 def kernel(
     stream_hbm, idx, cent, grad,
     stream,    emb, piece, logits, transport, half_sq, col_part, col_part2, col_vec,
-    row_vec, row_buf0, row_buf, row_sums, y_vec, y_buf0, y_buf, pot,
+    row_own, row_sib, row_chip, row_plane, pot,
     col_send0, col_send, col_buf0, col_buf,
     partial, long_out, short_out, long_in, short_in,
     emb_send, emb_recv, sib_send, sib_recv, z_send, z_recv,
-    row_send_sem, row_recv_sem, y_send_sem, y_recv_sem, col_send_sem, col_recv_sem,
+    row_sib_send, row_sib_recv, plane_send, plane_recv, col_send_sem, col_recv_sem,
     long_send_sem, long_recv_sem, short_send_sem, short_recv_sem, load_sem,
 ):
     dp = lax.axis_index("dp")
@@ -55,8 +63,8 @@
     def at_x(k):
         return {"dp": dp, "cent": lax.rem(x + k + NX, NX) * 2 + core}
 
-    def at_group(k):
-        return {"dp": dp, "cent": lax.rem(group + k, 2 * NX)}
+    def at_plane(ky, kx):
+        return {"dp": lax.rem(y + ky, NY) * NZ + z, "cent": lax.rem(x + kx, NX) * 2 + core}
 
     sibling = {"dp": dp, "cent": x * 2 + 1 - core}
 
@@ -133,12 +141,13 @@
         return slot
 
     piece[pl.ds(pl.multiple_of(z * OWN, OWN), OWN), :] = cent[...].astype(jnp.bfloat16)
-    load.wait()
-    first = gather(0)
     pl.semaphore_wait(barrier, 7)
     for h in (0, 1):
         send_piece(0, h, 1)
         send_piece(0, h, -1)
+    load.wait()
+    first = gather(0)
+    for h in (0, 1):
         send_half(first, h, at_y(1))
         send_half(first, h, at_y(-1))
     second = gather(2)
@@ -155,7 +164,9 @@
         if spread:
             send_half(slot, h, at_x(1))
             send_half(slot, h, at_x(-1))
-        if h:
+        if j:
+            send_half(slot, h, sibling)
+        elif h:
             send_block(slot, sibling)
 
     def on_block(k, j, forward=False):
@@ -177,14 +188,18 @@
             values = product[:, k * BLK:(k + 1) * BLK] - less
             logits[:, lanes] = values
             highest = jnp.max(values, axis=0, keepdims=True)
-            row_vec[0:1, lanes] = highest
-            row_vec[1:2, lanes] = jnp.sum(jnp.exp(values - highest), axis=0, keepdims=True)
+            total = jnp.sum(jnp.exp(values - highest), axis=0, keepdims=True)
+            row_own[0, pl.ds(blocks[k], 1), :] = highest + jnp.log(total)
 
     def score_from(offsets, c):
         blocks = [slot_of(k, c, j) for k, j in offsets]
         if offsets[0][0] and c is not core:
-            for slot in blocks:
-                wait_block(slot)
+            for (_, j), slot in zip(offsets, blocks):
+                if j % 2:
+                    for h in (0, 1):
+                        arrived(half_at(slot, h), emb_recv.at[slot, h])
+                else:
+                    wait_block(slot)
         score(blocks)
 
     own = [(0, 0), (0, 1), (0, 2), (0, 3)]
@@ -235,27 +250,29 @@
     score_from(late, core)
     score_from(late, other)
 
-    def exchange_group(src, bufs, which):
-        bufs[group] = src[...]
-        for k in range(1, 2 * NX):
-            send(
-                src, bufs.at[group],
-                row_send_sem.at[which, k - 1], row_recv_sem.at[which, group], at_group(k),
-            )
-        for k in range(1, 2 * NX):
-            other = lax.rem(group + k, 2 * NX)
-            arrived(bufs.at[other], row_recv_sem.at[which, other])
-
-    def exchange_y(src, bufs, which):
-        bufs[y] = src[...]
-        for k in range(1, NY):
-            send(
-                src, bufs.at[y],
-                y_send_sem.at[which, k - 1], y_recv_sem.at[which, y], at_y(k),
-            )
-        for k in range(1, NY):
-            other = lax.rem(y + k, NY)
-            arrived(bufs.at[other], y_recv_sem.at[which, other])
+    plane_peers = [(ky, kx) for ky in (2, 1, 3, 0) for kx in (2, 1, 3, 0) if ky or kx]
+
+    def exchange_rows(p, combine):
+        send(row_own.at[p], row_sib.at[p], row_sib_send.at[p], row_sib_recv.at[p], sibling)
+        arrived(row_sib.at[p], row_sib_recv.at[p])
+        chip = combine([row_own[p], row_sib[p]])
+        row_chip[p] = chip
+        me = y * NX + x
+        for at, (ky, kx) in enumerate(plane_peers):
+            send(row_chip.at[p], row_plane.at[p, me], plane_send.at[p, at], plane_recv.at[p, me], at_plane(ky, kx))
+        row_plane[p, me] = chip
+        for ky, kx in reversed(plane_peers):
+            peer = lax.rem(y + ky, NY) * NX + lax.rem(x + kx, NX)
+            arrived(row_plane.at[p, peer], plane_recv.at[p, peer])
+        return combine([row_plane[p, k] for k in range(PLANE)])
+
+    def log_sum(parts):
+        highest = functools.reduce(jnp.maximum, parts)
+        total = functools.reduce(jnp.add, [jnp.exp(part - highest) for part in parts])
+        return highest + jnp.log(total)
+
+    def plain_sum(parts):
+        return functools.reduce(jnp.add, parts)
 
     def start_z(src, bufs, which):
         for k in range(1, NZ):
@@ -295,27 +312,16 @@
     def to_columns(vec):
         return jnp.transpose(jnp.broadcast_to(vec, (BLK, COLS)))
 
-    exchange_group(row_vec, row_buf0, 0)
-    highest, total = merged(row_buf0, 2 * NX)
-    y_vec[0:1, :] = highest
-    y_vec[1:2, :] = total
-    exchange_y(y_vec, y_buf0, 0)
-    highest, total = merged(y_buf0, NY)
-    pot[...] = -(highest + jnp.log(total))
+    pot[...] = -exchange_rows(0, log_sum)
 
     def column_stats(g, carry):
         rows = pl.ds(pl.multiple_of(g * 16, 16), 16)
         tiles = [
-            logits[rows, k * BLK:(k + 1) * BLK] + pot[:, k * BLK:(k + 1) * BLK] for k in range(SLOTS)
+            logits[rows, k * BLK:(k + 1) * BLK] + pot[k:k + 1, :] for k in range(SLOTS)
         ]
-        highest = tiles[0]
-        for tile in tiles[1:]:
-            highest = jnp.maximum(highest, tile)
-        total = jnp.exp(tiles[0] - highest)
-        for tile in tiles[1:]:
-            total = total + jnp.exp(tile - highest)
+        highest = halving(jnp.maximum, tiles)
         col_part[rows, :] = highest
-        col_part2[rows, :] = total
+        col_part2[rows, :] = halving(jnp.add, [jnp.exp(tile - highest) for tile in tiles])
         return carry
 
     lax.fori_loop(0, COLS // 16, column_stats, 0)
@@ -328,43 +334,33 @@
     highest, total = merged(col_buf0, NZ)
     col_vec[...] = to_columns(BALANCE - (highest + jnp.log(total)))
 
-    WIDE = 2 * BLK
+    def lanes_of(t):
+        return pl.ds(pl.multiple_of(t * 4 * BLK, 4 * BLK), 4 * BLK)
+
+    def keep_sums(p, t, values):
+        sums = jnp.sum(values, axis=0, keepdims=True)
+        for u in range(4):
+            row_own[p, pl.ds(4 * t + u, 1), :] = sums[:, u * BLK:(u + 1) * BLK]
 
     def first_rows(t, carry):
-        lanes = pl.ds(pl.multiple_of(t * WIDE, WIDE), WIDE)
-        col = col_vec[...]
-        both = jnp.concatenate([col, col], axis=1)
-        plan = jnp.exp(logits[:, lanes] + pot[:, lanes] + both)
-        logits[:, lanes] = plan
-        row_sums[:, lanes] = jnp.sum(plan, axis=0, keepdims=True)
+        row = jnp.concatenate([pot[pl.ds(4 * t + u, 1), :] for u in range(4)], axis=1)
+        plan = jnp.exp(logits[:, lanes_of(t)] + row + jnp.concatenate([col_vec[...]] * 4, axis=1))
+        logits[:, lanes_of(t)] = plan
+        keep_sums(1, t, plan)
         return carry
 
-    def later_rows(t, carry):
-        lanes = pl.ds(pl.multiple_of(t * WIDE, WIDE), WIDE)
-        col = col_vec[...]
-        both = jnp.concatenate([col, col], axis=1)
-        row_sums[:, lanes] = jnp.sum(logits[:, lanes] * both, axis=0, keepdims=True)
-        return carry
-
-    def row_factor(which):
-        row_vec1 = row_buf.at[which - 1]
-        y_bufs = y_buf.at[which - 1]
-        src = row_src.at[which - 1]
-        src[...] = row_sums[...]
-        exchange_group(src, row_vec1, which)
-        mid = y_src.at[which - 1]
-        mid[...] = added(row_vec1, 2 * NX)
-        exchange_y(mid, y_bufs, which)
-        pot[...] = 1.0 / added(y_bufs, NY)
-
-    row_src = row_buf.at[:, 2 * NX]
-    y_src = y_buf.at[:, NY]
+    def later_rows(p):
+        def body(t, carry):
+            keep_sums(p, t, logits[:, lanes_of(t)] * jnp.concatenate([col_vec[...]] * 4, axis=1))
+            return carry
+
+        lax.fori_loop(0, SLOTS // 4, body, 0)
 
     def column_sums(g, carry):
-        rows = pl.ds(pl.multiple_of(g * 32, 32), 32)
-        total = logits[rows, 0:BLK] * pot[:, 0:BLK]
+        rows = pl.ds(pl.multiple_of(g * 64, 64), 64)
+        total = logits[rows, 0:BLK] * pot[0:1, :]
         for k in range(1, SLOTS):
-            total = total + logits[rows, k * BLK:(k + 1) * BLK] * pot[:, k * BLK:(k + 1) * BLK]
+            total = total + logits[rows, k * BLK:(k + 1) * BLK] * pot[k:k + 1, :]
         col_part[rows, :] = total
         return carry
 
@@ -377,49 +373,46 @@
         finish_z(col_buf.at[which - 1], which)
         return added(col_buf.at[which - 1], NZ)
 
-    lax.fori_loop(0, NR // WIDE, first_rows, 0)
-    row_factor(1)
+    lax.fori_loop(0, SLOTS // 4, first_rows, 0)
+    pot[...] = 1.0 / exchange_rows(1, plain_sum)
     for sweep in (1, 2):
-        lax.fori_loop(0, COLS // 32, column_sums, 0)
+        lax.fori_loop(0, COLS // 64, column_sums, 0)
         start_total(sweep)
         col_vec[...] = to_columns((ROWS / KB) / finish_total(sweep))
-        lax.fori_loop(0, NR // WIDE, later_rows, 0)
-        row_factor(sweep + 1)
-
-    def make_transport(g, carry):
-        rows = pl.ds(pl.multiple_of(g * 32, 32), 32)
-        col = col_vec[rows, :]
-        mass = jnp.zeros((32, BLK), jnp.float32)
-        for k in range(SLOTS):
-            lanes = slice(k * BLK, (k + 1) * BLK)
-            rounded = (logits[rows, lanes] * pot[:, lanes] * col).astype(jnp.bfloat16)
-            transport[rows, lanes] = rounded
-            mass = mass + rounded.astype(jnp.float32)
-        col_part[rows, :] = mass
-        return carry
-
-    lax.fori_loop(0, COLS // 32, make_transport, 0)
-
-    def weigh(d0, d1):
+        later_rows(sweep + 1)
+        pot[...] = 1.0 / exchange_rows(sweep + 1, plain_sum)
+
+    def make_transport(d):
+        def body(g, carry):
+            start = lax.rem(z + d + NZ, NZ) * OWN + g * 32
+            rows = pl.ds(pl.multiple_of(start, 32), 32)
+            col = col_vec[rows, :]
+            mass = jnp.zeros((32, BLK), jnp.float32)
+            for k in range(SLOTS):
+                lanes = slice(k * BLK, (k + 1) * BLK)
+                rounded = (logits[rows, lanes] * pot[k:k + 1, :] * col).astype(jnp.bfloat16)
+                transport[rows, lanes] = rounded
+                mass = mass + rounded.astype(jnp.float32)
+            col_part[rows, :] = mass
+            return carry
+
+        lax.fori_loop(0, OWN // 32, body, 0)
+
+    def weigh(d0, d1, n):
         def rows_of(d):
             return transport[pl.ds(pl.multiple_of(lax.rem(z + d + NZ, NZ) * OWN, OWN), OWN), :]
 
         left = jnp.concatenate([rows_of(d0), rows_of(d1)], axis=0)
-
-        def body(n, carry):
-            lanes = pl.ds(pl.multiple_of(n * 256, 256), 256)
-            both = jnp.dot(left, emb[:, lanes], preferred_element_type=jnp.float32)
-            partial[d0 % NZ, :, lanes] = both[:OWN]
-            partial[d1 % NZ, :, lanes] = both[OWN:]
-            return carry
-
-        lax.fori_loop(0, E // 256, body, 0)
+        lanes = slice(n * 2 * CHUNK, (n + 1) * 2 * CHUNK)
+        both = jnp.dot(left, emb[:, lanes], preferred_element_type=jnp.float32)
+        partial[d0 % NZ, :, lanes] = both[:OWN]
+        partial[d1 % NZ, :, lanes] = both[OWN:]
 
     def features(h):
-        return slice(h * HALF, (h + 1) * HALF)
+        return slice(h * CHUNK, (h + 1) * CHUNK)
 
     def long_step(h, s):
-        way = 1 - 2 * h
+        way = 1 - 2 * (h % 2)
         value = partial[(way * (4 - s)) % NZ, :, features(h)]
         if s:
             arrived(long_in.at[h * 4 + s - 1], long_recv_sem.at[h * 4 + s - 1])
@@ -429,7 +422,7 @@
         send(long_out.at[at], long_in.at[at], long_send_sem.at[at], long_recv_sem.at[at], at_z(way))
 
     def short_step(h, s):
-        way = 2 * h - 1
+        way = 2 * (h % 2) - 1
         value = partial[(way * (3 - s)) % NZ, :, features(h)]
         if s:
             arrived(short_in.at[h * 3 + s - 1], short_recv_sem.at[h * 3 + s - 1])
@@ -438,28 +431,42 @@
         short_out[at] = value.astype(SUM_TYPE)
         send(short_out.at[at], short_in.at[at], short_send_sem.at[at], short_recv_sem.at[at], at_z(way))
 
+    make_transport(4)
+    make_transport(3)
+    for n in range(CHUNKS // 2):
+        weigh(4, 3, n)
+        for h in (2 * n, 2 * n + 1):
+            long_step(h, 0)
+        short_step(2 * n + 1, 0)
+    make_transport(-3)
+    make_transport(2)
+    for n in range(CHUNKS // 2):
+        weigh(-3, 2, n)
+        short_step(2 * n, 0)
+    for h in range(CHUNKS):
+        long_step(h, 1)
+        if h % 2:
+            short_step(h, 1)
+    make_transport(-2)
+    make_transport(1)
+    for n in range(CHUNKS // 2):
+        weigh(-2, 1, n)
+    for n in range(CHUNKS // 2):
+        short_step(2 * n, 1)
+        for h in (2 * n, 2 * n + 1):
+            long_step(h, 2)
+        short_step(2 * n + 1, 2)
+    make_transport(-1)
+    make_transport(0)
     start_total(3)
-    weigh(4, 3)
-    long_step(0, 0)
-    long_step(1, 0)
-    short_step(1, 0)
-    weigh(-3, 2)
-    short_step(0, 0)
-    weigh(-2, 1)
-    long_step(0, 1)
-    long_step(1, 1)
-    short_step(0, 1)
-    short_step(1, 1)
-    weigh(-1, 0)
-    long_step(0, 2)
-    long_step(1, 2)
-    short_step(0, 2)
-    short_step(1, 2)
-    long_step(0, 3)
-    long_step(1, 3)
+    for n in range(CHUNKS // 2):
+        weigh(-1, 0, n)
+        short_step(2 * n, 2)
+    for h in range(CHUNKS):
+        long_step(h, 3)
     col_vec[...] = to_columns(finish_total(3))
     mass = col_vec[pl.ds(pl.multiple_of(z * OWN, OWN), OWN), :][:, :1]
-    for h in (0, 1):
+    for h in range(CHUNKS):
         arrived(short_in.at[h * 3 + 2], short_recv_sem.at[h * 3 + 2])
         weighted = partial[0, :, features(h)] + short_in[h * 3 + 2].astype(jnp.float32)
         arrived(long_in.at[h * 4 + 3], long_recv_sem.at[h * 4 + 3])
@@ -482,39 +489,36 @@
         pltpu.VMEM((COLS, BLK), f32),
         pltpu.VMEM((COLS, BLK), f32),
         pltpu.VMEM((COLS, BLK), f32),
-        pltpu.VMEM((2, NR), f32),
-        pltpu.VMEM((2 * NX, 2, NR), f32),
-        pltpu.VMEM((3, 2 * NX + 1, 1, NR), f32),
-        pltpu.VMEM((1, NR), f32),
-        pltpu.VMEM((2, NR), f32),
-        pltpu.VMEM((NY, 2, NR), f32),
-        pltpu.VMEM((3, NY + 1, 1, NR), f32),
-        pltpu.VMEM((1, NR), f32),
+        pltpu.VMEM((4, SLOTS, BLK), f32),
+        pltpu.VMEM((4, SLOTS, BLK), f32),
+        pltpu.VMEM((4, SLOTS, BLK), f32),
+        pltpu.VMEM((4, PLANE, SLOTS, BLK), f32),
+        pltpu.VMEM((SLOTS, BLK), f32),
         pltpu.VMEM((2, COLS), f32),
         pltpu.VMEM((3, 1, COLS), f32),
         pltpu.VMEM((NZ, 2, COLS), f32),
         pltpu.VMEM((3, NZ, 1, COLS), f32),
         pltpu.VMEM((NZ, OWN, E), f32),
-        pltpu.VMEM((8, OWN, HALF), SUM_TYPE),
-        pltpu.VMEM((6, OWN, HALF), SUM_TYPE),
-        pltpu.VMEM((8, OWN, HALF), SUM_TYPE),
-        pltpu.VMEM((6, OWN, HALF), SUM_TYPE),
+        pltpu.VMEM((4 * CHUNKS, OWN, CHUNK), SUM_TYPE),
+        pltpu.VMEM((3 * CHUNKS, OWN, CHUNK), SUM_TYPE),
+        pltpu.VMEM((4 * CHUNKS, OWN, CHUNK), SUM_TYPE),
+        pltpu.VMEM((3 * CHUNKS, OWN, CHUNK), SUM_TYPE),
         pltpu.SemaphoreType.DMA((40,)),
         pltpu.SemaphoreType.DMA((SLOTS, 2)),
         pltpu.SemaphoreType.DMA,
         pltpu.SemaphoreType.DMA,
         pltpu.SemaphoreType.DMA((14,)),
         pltpu.SemaphoreType.DMA((NZ, 2)),
-        pltpu.SemaphoreType.DMA((4, 2 * NX - 1)),
-        pltpu.SemaphoreType.DMA((4, 2 * NX)),
-        pltpu.SemaphoreType.DMA((4, NY - 1)),
-        pltpu.SemaphoreType.DMA((4, NY)),
+        pltpu.SemaphoreType.DMA((4,)),
+        pltpu.SemaphoreType.DMA((4,)),
+        pltpu.SemaphoreType.DMA((4, PLANE - 1)),
+        pltpu.SemaphoreType.DMA((4, PLANE)),
         pltpu.SemaphoreType.DMA((4, NZ - 1)),
         pltpu.SemaphoreType.DMA((4, NZ)),
-        pltpu.SemaphoreType.DMA((8,)),
-        pltpu.SemaphoreType.DMA((8,)),
-        pltpu.SemaphoreType.DMA((6,)),
-        pltpu.SemaphoreType.DMA((6,)),
+        pltpu.SemaphoreType.DMA((4 * CHUNKS,)),
+        pltpu.SemaphoreType.DMA((4 * CHUNKS,)),
+        pltpu.SemaphoreType.DMA((3 * CHUNKS,)),
+        pltpu.SemaphoreType.DMA((3 * CHUNKS,)),
         pltpu.SemaphoreType.DMA,
     ]
     gradient = pl.pallas_call(

time: 112 us -> 103 us (0.920)
  Pallas kernels: 109 us -> 99.5 us
    pallas_call x1, Pallas kernels: 109 us -> 99.5 us  [per_device(): pl.pallas_call(kernel, out_shape=jax.ShapeDtypeStruct((OWN, E), f32), in_...]
where the time goes in v3:
time: 103 us; the launch traced here: 102 us
  Pallas kernels  99.5 us (97%)
  other arithmetic  1.79 us (2%)
    pallas_call x1, Pallas kernels, per_device(): pl.pallas_call(kernel, out_shape=jax.ShapeDtypeStruct((OWN, E), f32), in_...  99.5 us

profile of v3, /device:TPU:8, one launch (start us, length us, event | category | flops | bytes accessed | tf_op | source)
XLA Modules:
  0.0 102.0 jit_solution(2643868401597324855)
XLA Ops:
  0.6 0.0 copy-start
  0.6 0.0 copy-start.1
  0.7 0.0 copy-start.2
  0.7 99.5 %balanced_kmeans.1 = f32[64,768]{1,0:T(8,128)} custom-call(bf16[2048,768]{1,0:T(8,128)(2,1)} %stream_hbm.1, s32[8,128]{1,0:T(8,128)} %bitcast.1, f32[64,768]{1,0:T(8,128)} %cent.1), custom_call_target="tpu_custom_call" | custom-call | flops 6442450944 | bytes 4194304 | tf_op jit(solution)/shard_map/balanced_kmeans/pallas_call | solution.py:524
  100.2 0.0 copy-done
  100.2 0.0 copy-done.1
  100.2 0.0 copy-done.2
  100.2 1.8 %divide_subtract_fusion = (f32[64,768]{1,0:T(8,128)}, f32[64,768]{1,0:T(8,128)}, f32[64,768]{1,0:T(8,128)}) fusion(f32[64,768]{1,0:T(8,128)S(1)} %copy-done, f32[64,768]{1,0:T(8,128)} %balanced_kmeans.1, f32[64,768]{1,0:T(8,128)S(1)} %copy-done.1, f32[64,768]{1,0:T(8,128)S(1)} %copy-done.2), kind=kLoop, calls=%fused_computation.2 | loop fusion | flops 540672 | bytes 1376256 | tf_op jit(solution)/shard_map/sub | solution.py:540
Async XLA Ops:
  0.6 99.6 %copy-start = (f32[64,768]{1,0:T(8,128)S(1)}, f32[64,768]{1,0:T(8,128)}, u32[]{:S(2)}) copy-start(f32[64,768]{1,0:T(8,128)} %cent.1) | copy-start | bytes 589828
  0.6 99.6 %copy-start.1 = (f32[64,768]{1,0:T(8,128)S(1)}, f32[64,768]{1,0:T(8,128)}, u32[]{:S(2)}) copy-start(f32[64,768]{1,0:T(8,128)} %param.8) | copy-start | bytes 589828
  0.7 99.6 %copy-start.2 = (f32[64,768]{1,0:T(8,128)S(1)}, f32[64,768]{1,0:T(8,128)}, u32[]{:S(2)}) copy-start(f32[64,768]{1,0:T(8,128)} %param.9) | copy-start | bytes 589828

commit v4 on v3

--- a/solution.py
+++ b/solution.py
@@ -18,6 +18,7 @@
 COLS = OWN * NZ
 ND = 1024
 BLK = 128
+PARTS = 2
 SLOTS = NY * ND // BLK
 NR = SLOTS * BLK
 STREAM = 2 * ND
@@ -105,11 +106,11 @@
     def wait_block(slot):
         arrived(emb_at(slot), emb_recv.at[slot, 0])
 
-    def half_at(slot, h):
-        return emb.at[pl.ds(pl.multiple_of(slot * BLK + h * (BLK // 2), BLK // 2), BLK // 2), :]
-
-    def send_half(slot, h, device):
-        send(half_at(slot, h), half_at(slot, h), emb_send.at[sends[0]], emb_recv.at[slot, h], device)
+    def part_at(slot, h):
+        return emb.at[pl.ds(pl.multiple_of(slot * BLK + h * (BLK // PARTS), BLK // PARTS), BLK // PARTS), :]
+
+    def send_part(slot, h, device):
+        send(part_at(slot, h), part_at(slot, h), emb_send.at[sends[0]], emb_recv.at[slot, h], device)
         sends[0] += 1
 
     def piece_at(k, h):
@@ -141,32 +142,30 @@
         return slot
 
     piece[pl.ds(pl.multiple_of(z * OWN, OWN), OWN), :] = cent[...].astype(jnp.bfloat16)
+    load.wait()
+    first = gather(0)
     pl.semaphore_wait(barrier, 7)
+    for h in range(PARTS):
+        send_part(first, h, at_y(1))
+        send_part(first, h, at_y(-1))
     for h in (0, 1):
         send_piece(0, h, 1)
         send_piece(0, h, -1)
-    load.wait()
-    first = gather(0)
-    for h in (0, 1):
-        send_half(first, h, at_y(1))
-        send_half(first, h, at_y(-1))
     second = gather(2)
     gather(1)
     gather(3)
     own_first = y * 8 + core * 4
     send(emb_at(own_first, 4), emb_at(own_first, 4), sib_send, sib_recv, sibling)
 
-    def on_half(k, j, h, forward=False, spread=False):
+    def on_part(k, j, h, forward=False, spread=False):
         slot = slot_of(k, core, j)
-        arrived(half_at(slot, h), emb_recv.at[slot, h])
+        arrived(part_at(slot, h), emb_recv.at[slot, h])
         if forward:
-            send_half(slot, h, at_y(1))
+            send_part(slot, h, at_y(1))
         if spread:
-            send_half(slot, h, at_x(1))
-            send_half(slot, h, at_x(-1))
-        if j:
-            send_half(slot, h, sibling)
-        elif h:
+            send_part(slot, h, at_x(1))
+            send_part(slot, h, at_x(-1))
+        if h == PARTS - 1:
             send_block(slot, sibling)
 
     def on_block(k, j, forward=False):
@@ -194,12 +193,8 @@
     def score_from(offsets, c):
         blocks = [slot_of(k, c, j) for k, j in offsets]
         if offsets[0][0] and c is not core:
-            for (_, j), slot in zip(offsets, blocks):
-                if j % 2:
-                    for h in (0, 1):
-                        arrived(half_at(slot, h), emb_recv.at[slot, h])
-                else:
-                    wait_block(slot)
+            for slot in blocks:
+                wait_block(slot)
         score(blocks)
 
     own = [(0, 0), (0, 1), (0, 2), (0, 3)]
@@ -209,23 +204,24 @@
     other = 1 - core
 
     on_pieces(1, 0)
-    on_half(-1, 0, 0, forward=True, spread=True)
-    on_half(1, 0, 0, spread=True)
-    on_pieces(1, 1)
-    on_half(-1, 0, 1, forward=True, spread=True)
-    on_half(1, 0, 1, spread=True)
+    for h in range(PARTS):
+        on_part(-1, 0, h, forward=True, spread=True)
+        on_part(1, 0, h, spread=True)
+        if h == PARTS // 2 - 1:
+            on_pieces(1, 1)
+            send_block(second, at_y(-1))
     send_block(second, at_y(1))
-    send_block(second, at_y(-1))
     on_pieces(2, 0)
     on_pieces(2, 1)
-    on_half(2, 0, 0, spread=True)
-    on_pieces(3, 0, False)
-    on_half(2, 0, 1, spread=True)
+    for h in range(PARTS):
+        on_part(2, 0, h, spread=True)
+        if h == PARTS // 2 - 1:
+            on_pieces(3, 0, False)
     on_pieces(3, 1, False)
     on_block(1, 2, forward=True)
-    for h in (0, 1):
-        on_half(-1, 1, h)
-        on_half(-1, 3, h)
+    for h in range(PARTS):
+        on_part(-1, 1, h)
+        on_part(-1, 3, h)
     for h in (0, 1):
         arrived(piece_at(-4, h), z_recv.at[lax.rem(z + 4, NZ), h])
     whole = piece[...].astype(jnp.float32)
@@ -236,16 +232,16 @@
     score_from(early, core)
     arrived(emb_at(y * 8 + other * 4, 4), sib_recv)
     score_from(own, other)
-    for h in (0, 1):
-        on_half(1, 1, h)
-        on_half(1, 3, h)
+    for h in range(PARTS):
+        on_part(1, 1, h)
+        on_part(1, 3, h)
     on_block(-1, 2)
     score_from(early, other)
     score_from(middle, core)
     on_block(2, 2)
-    for h in (0, 1):
-        on_half(2, 1, h)
-        on_half(2, 3, h)
+    for h in range(PARTS):
+        on_part(2, 1, h)
+        on_part(2, 3, h)
     score_from(middle, other)
     score_from(late, core)
     score_from(late, other)
@@ -320,8 +316,11 @@
             logits[rows, k * BLK:(k + 1) * BLK] + pot[k:k + 1, :] for k in range(SLOTS)
         ]
         highest = halving(jnp.maximum, tiles)
+        tiles = [jnp.exp(tile - highest) for tile in tiles]
+        for k, tile in enumerate(tiles):
+            logits[rows, k * BLK:(k + 1) * BLK] = tile
         col_part[rows, :] = highest
-        col_part2[rows, :] = halving(jnp.add, [jnp.exp(tile - highest) for tile in tiles])
+        col_part2[rows, :] = halving(jnp.add, tiles)
         return carry
 
     lax.fori_loop(0, COLS // 16, column_stats, 0)
@@ -332,7 +331,8 @@
     col_send0[1:2, :] = jnp.sum(sums * jnp.exp(peaks - highest), axis=0, keepdims=True)
     exchange_z(col_send0, col_buf0, 0)
     highest, total = merged(col_buf0, NZ)
-    col_vec[...] = to_columns(BALANCE - (highest + jnp.log(total)))
+    half_sq[...] = jnp.exp(col_part[...] + to_columns(BALANCE - (highest + jnp.log(total))))
+    col_vec[...] = half_sq[...]
 
     def lanes_of(t):
         return pl.ds(pl.multiple_of(t * 4 * BLK, 4 * BLK), 4 * BLK)
@@ -341,13 +341,6 @@
         sums = jnp.sum(values, axis=0, keepdims=True)
         for u in range(4):
             row_own[p, pl.ds(4 * t + u, 1), :] = sums[:, u * BLK:(u + 1) * BLK]
-
-    def first_rows(t, carry):
-        row = jnp.concatenate([pot[pl.ds(4 * t + u, 1), :] for u in range(4)], axis=1)
-        plan = jnp.exp(logits[:, lanes_of(t)] + row + jnp.concatenate([col_vec[...]] * 4, axis=1))
-        logits[:, lanes_of(t)] = plan
-        keep_sums(1, t, plan)
-        return carry
 
     def later_rows(p):
         def body(t, carry):
@@ -361,7 +354,7 @@
         total = logits[rows, 0:BLK] * pot[0:1, :]
         for k in range(1, SLOTS):
             total = total + logits[rows, k * BLK:(k + 1) * BLK] * pot[k:k + 1, :]
-        col_part[rows, :] = total
+        col_part[rows, :] = total * half_sq[rows, :]
         return carry
 
     def start_total(which):
@@ -373,12 +366,12 @@
         finish_z(col_buf.at[which - 1], which)
         return added(col_buf.at[which - 1], NZ)
 
-    lax.fori_loop(0, SLOTS // 4, first_rows, 0)
+    later_rows(1)
     pot[...] = 1.0 / exchange_rows(1, plain_sum)
     for sweep in (1, 2):
         lax.fori_loop(0, COLS // 64, column_sums, 0)
         start_total(sweep)
-        col_vec[...] = to_columns((ROWS / KB) / finish_total(sweep))
+        col_vec[...] = half_sq[...] * to_columns((ROWS / KB) / finish_total(sweep))
         later_rows(sweep + 1)
         pot[...] = 1.0 / exchange_rows(sweep + 1, plain_sum)
 
@@ -503,8 +496,8 @@
         pltpu.VMEM((3 * CHUNKS, OWN, CHUNK), SUM_TYPE),
         pltpu.VMEM((4 * CHUNKS, OWN, CHUNK), SUM_TYPE),
         pltpu.VMEM((3 * CHUNKS, OWN, CHUNK), SUM_TYPE),
-        pltpu.SemaphoreType.DMA((40,)),
-        pltpu.SemaphoreType.DMA((SLOTS, 2)),
+        pltpu.SemaphoreType.DMA((64,)),
+        pltpu.SemaphoreType.DMA((SLOTS, PARTS)),
         pltpu.SemaphoreType.DMA,
         pltpu.SemaphoreType.DMA,
         pltpu.SemaphoreType.DMA((14,)),

time: 103 us -> 102 us (level)
  no operation moved by 1% of the time
where the time goes in v4:
time: 102 us
  Pallas kernels  99.3 us (97%)
  other arithmetic  1.79 us (2%)
    pallas_call x1, Pallas kernels, per_device(): pl.pallas_call(kernel, out_shape=jax.ShapeDtypeStruct((OWN, E), f32), in_...  99.3 us

profile of v4, /device:TPU:8, one launch (start us, length us, event | category | flops | bytes accessed | tf_op | source)
XLA Modules:
  0.0 101.8 jit_solution(752908700174645852)
XLA Ops:
  0.6 0.0 copy-start
  0.6 0.0 copy-start.1
  0.7 0.0 copy-start.2
  0.7 99.3 %balanced_kmeans.1 = f32[64,768]{1,0:T(8,128)} custom-call(bf16[2048,768]{1,0:T(8,128)(2,1)} %stream_hbm.1, s32[8,128]{1,0:T(8,128)} %bitcast.1, f32[64,768]{1,0:T(8,128)} %cent.1), custom_call_target="tpu_custom_call" | custom-call | flops 6442450944 | bytes 4194304 | tf_op jit(solution)/shard_map/balanced_kmeans/pallas_call | solution.py:517
  100.0 0.0 copy-done
  100.0 0.0 copy-done.1
  100.0 0.0 copy-done.2
  100.0 1.8 %divide_subtract_fusion = (f32[64,768]{1,0:T(8,128)}, f32[64,768]{1,0:T(8,128)}, f32[64,768]{1,0:T(8,128)}) fusion(f32[64,768]{1,0:T(8,128)S(1)} %copy-done, f32[64,768]{1,0:T(8,128)} %balanced_kmeans.1, f32[64,768]{1,0:T(8,128)S(1)} %copy-done.1, f32[64,768]{1,0:T(8,128)S(1)} %copy-done.2), kind=kLoop, calls=%fused_computation.2 | loop fusion | flops 540672 | bytes 1376256 | tf_op jit(solution)/shard_map/sub | solution.py:533
Async XLA Ops:
  0.6 99.4 %copy-start = (f32[64,768]{1,0:T(8,128)S(1)}, f32[64,768]{1,0:T(8,128)}, u32[]{:S(2)}) copy-start(f32[64,768]{1,0:T(8,128)} %cent.1) | copy-start | bytes 589828
  0.6 99.4 %copy-start.1 = (f32[64,768]{1,0:T(8,128)S(1)}, f32[64,768]{1,0:T(8,128)}, u32[]{:S(2)}) copy-start(f32[64,768]{1,0:T(8,128)} %param.8) | copy-start | bytes 589828
  0.7 99.4 %copy-start.2 = (f32[64,768]{1,0:T(8,128)S(1)}, f32[64,768]{1,0:T(8,128)}, u32[]{:S(2)}) copy-start(f32[64,768]{1,0:T(8,128)} %param.9) | copy-start | bytes 589828

commit v5 on v4

--- a/solution.py
+++ b/solution.py
@@ -335,22 +335,22 @@
     col_vec[...] = half_sq[...]
 
     def lanes_of(t):
-        return pl.ds(pl.multiple_of(t * 4 * BLK, 4 * BLK), 4 * BLK)
+        return pl.ds(pl.multiple_of(t * 8 * BLK, 8 * BLK), 8 * BLK)
 
     def keep_sums(p, t, values):
         sums = jnp.sum(values, axis=0, keepdims=True)
-        for u in range(4):
-            row_own[p, pl.ds(4 * t + u, 1), :] = sums[:, u * BLK:(u + 1) * BLK]
+        for u in range(8):
+            row_own[p, pl.ds(8 * t + u, 1), :] = sums[:, u * BLK:(u + 1) * BLK]
 
     def later_rows(p):
         def body(t, carry):
-            keep_sums(p, t, logits[:, lanes_of(t)] * jnp.concatenate([col_vec[...]] * 4, axis=1))
+            keep_sums(p, t, logits[:, lanes_of(t)] * jnp.concatenate([col_vec[...]] * 8, axis=1))
             return carry
 
-        lax.fori_loop(0, SLOTS // 4, body, 0)
+        lax.fori_loop(0, SLOTS // 8, body, 0)
 
     def column_sums(g, carry):
-        rows = pl.ds(pl.multiple_of(g * 64, 64), 64)
+        rows = pl.ds(pl.multiple_of(g * 128, 128), 128)
         total = logits[rows, 0:BLK] * pot[0:1, :]
         for k in range(1, SLOTS):
             total = total + logits[rows, k * BLK:(k + 1) * BLK] * pot[k:k + 1, :]
@@ -369,7 +369,7 @@
     later_rows(1)
     pot[...] = 1.0 / exchange_rows(1, plain_sum)
     for sweep in (1, 2):
-        lax.fori_loop(0, COLS // 64, column_sums, 0)
+        lax.fori_loop(0, COLS // 128, column_sums, 0)
         start_total(sweep)
         col_vec[...] = half_sq[...] * to_columns((ROWS / KB) / finish_total(sweep))
         later_rows(sweep + 1)

time: 102 us -> 101 us (level)
  no operation moved by 1% of the time
where the time goes in v5:
time: 101 us
  Pallas kernels  98.5 us (98%)
  other arithmetic  1.79 us (2%)
    pallas_call x1, Pallas kernels, per_device(): pl.pallas_call(kernel, out_shape=jax.ShapeDtypeStruct((OWN, E), f32), in_...  98.5 us

profile of v5, /device:TPU:8, one launch (start us, length us, event | category | flops | bytes accessed | tf_op | source)
XLA Modules:
  0.0 101.0 jit_solution(4210851544229090917)
XLA Ops:
  0.6 0.0 copy-start
  0.6 0.0 copy-start.1
  0.7 0.0 copy-start.2
  0.7 98.5 %balanced_kmeans.1 = f32[64,768]{1,0:T(8,128)} custom-call(bf16[2048,768]{1,0:T(8,128)(2,1)} %stream_hbm.1, s32[8,128]{1,0:T(8,128)} %bitcast.1, f32[64,768]{1,0:T(8,128)} %cent.1), custom_call_target="tpu_custom_call" | custom-call | flops 6442450944 | bytes 4194304 | tf_op jit(solution)/shard_map/balanced_kmeans/pallas_call | solution.py:517
  99.2 0.0 copy-done
  99.2 0.0 copy-done.1
  99.2 0.0 copy-done.2
  99.2 1.8 %divide_subtract_fusion = (f32[64,768]{1,0:T(8,128)}, f32[64,768]{1,0:T(8,128)}, f32[64,768]{1,0:T(8,128)}) fusion(f32[64,768]{1,0:T(8,128)S(1)} %copy-done, f32[64,768]{1,0:T(8,128)} %balanced_kmeans.1, f32[64,768]{1,0:T(8,128)S(1)} %copy-done.1, f32[64,768]{1,0:T(8,128)S(1)} %copy-done.2), kind=kLoop, calls=%fused_computation.2 | loop fusion | flops 540672 | bytes 1376256 | tf_op jit(solution)/shard_map/sub | solution.py:533
Async XLA Ops:
  0.6 98.5 %copy-start = (f32[64,768]{1,0:T(8,128)S(1)}, f32[64,768]{1,0:T(8,128)}, u32[]{:S(2)}) copy-start(f32[64,768]{1,0:T(8,128)} %cent.1) | copy-start | bytes 589828
  0.6 98.5 %copy-start.1 = (f32[64,768]{1,0:T(8,128)S(1)}, f32[64,768]{1,0:T(8,128)}, u32[]{:S(2)}) copy-start(f32[64,768]{1,0:T(8,128)} %param.8) | copy-start | bytes 589828
  0.7 98.5 %copy-start.2 = (f32[64,768]{1,0:T(8,128)S(1)}, f32[64,768]{1,0:T(8,128)}, u32[]{:S(2)}) copy-start(f32[64,768]{1,0:T(8,128)} %param.9) | copy-start | bytes 589828

commit v6 on v5

--- a/solution.py
+++ b/solution.py
@@ -311,7 +311,7 @@
     pot[...] = -exchange_rows(0, log_sum)
 
     def column_stats(g, carry):
-        rows = pl.ds(pl.multiple_of(g * 16, 16), 16)
+        rows = pl.ds(pl.multiple_of(g * 32, 32), 32)
         tiles = [
             logits[rows, k * BLK:(k + 1) * BLK] + pot[k:k + 1, :] for k in range(SLOTS)
         ]
@@ -323,7 +323,7 @@
         col_part2[rows, :] = halving(jnp.add, tiles)
         return carry
 
-    lax.fori_loop(0, COLS // 16, column_stats, 0)
+    lax.fori_loop(0, COLS // 32, column_stats, 0)
     peaks = to_lanes(col_part[...])
     sums = to_lanes(col_part2[...])
     highest = jnp.max(peaks, axis=0, keepdims=True)
@@ -350,7 +350,7 @@
         lax.fori_loop(0, SLOTS // 8, body, 0)
 
     def column_sums(g, carry):
-        rows = pl.ds(pl.multiple_of(g * 128, 128), 128)
+        rows = pl.ds(pl.multiple_of(g * 256, 256), 256)
         total = logits[rows, 0:BLK] * pot[0:1, :]
         for k in range(1, SLOTS):
             total = total + logits[rows, k * BLK:(k + 1) * BLK] * pot[k:k + 1, :]
@@ -369,7 +369,7 @@
     later_rows(1)
     pot[...] = 1.0 / exchange_rows(1, plain_sum)
     for sweep in (1, 2):
-        lax.fori_loop(0, COLS // 128, column_sums, 0)
+        lax.fori_loop(0, COLS // 256, column_sums, 0)
         start_total(sweep)
         col_vec[...] = half_sq[...] * to_columns((ROWS / KB) / finish_total(sweep))
         later_rows(sweep + 1)

time: 101 us -> 101 us (level)
  no operation moved by 1% of the time
where the time goes in v6:
time: 101 us
  Pallas kernels  98.1 us (97%)
  other arithmetic  1.79 us (2%)
    pallas_call x1, Pallas kernels, per_device(): pl.pallas_call(kernel, out_shape=jax.ShapeDtypeStruct((OWN, E), f32), in_...  98.1 us

profile of v6, /device:TPU:8, one launch (start us, length us, event | category | flops | bytes accessed | tf_op | source)
XLA Modules:
  0.0 100.6 jit_solution(6123904972979803672)
XLA Ops:
  0.6 0.0 copy-start
  0.6 0.0 copy-start.1
  0.7 0.0 copy-start.2
  0.7 98.1 %balanced_kmeans.1 = f32[64,768]{1,0:T(8,128)} custom-call(bf16[2048,768]{1,0:T(8,128)(2,1)} %stream_hbm.1, s32[8,128]{1,0:T(8,128)} %bitcast.1, f32[64,768]{1,0:T(8,128)} %cent.1), custom_call_target="tpu_custom_call" | custom-call | flops 6442450944 | bytes 4194304 | tf_op jit(solution)/shard_map/balanced_kmeans/pallas_call | solution.py:517
  98.7 0.0 copy-done
  98.7 0.0 copy-done.1
  98.8 0.0 copy-done.2
  98.8 1.8 %divide_subtract_fusion = (f32[64,768]{1,0:T(8,128)}, f32[64,768]{1,0:T(8,128)}, f32[64,768]{1,0:T(8,128)}) fusion(f32[64,768]{1,0:T(8,128)S(1)} %copy-done, f32[64,768]{1,0:T(8,128)} %balanced_kmeans.1, f32[64,768]{1,0:T(8,128)S(1)} %copy-done.1, f32[64,768]{1,0:T(8,128)S(1)} %copy-done.2), kind=kLoop, calls=%fused_computation.2 | loop fusion | flops 540672 | bytes 1376256 | tf_op jit(solution)/shard_map/sub | solution.py:533
Async XLA Ops:
  0.6 98.1 %copy-start = (f32[64,768]{1,0:T(8,128)S(1)}, f32[64,768]{1,0:T(8,128)}, u32[]{:S(2)}) copy-start(f32[64,768]{1,0:T(8,128)} %cent.1) | copy-start | bytes 589828
  0.6 98.1 %copy-start.1 = (f32[64,768]{1,0:T(8,128)S(1)}, f32[64,768]{1,0:T(8,128)}, u32[]{:S(2)}) copy-start(f32[64,768]{1,0:T(8,128)} %param.8) | copy-start | bytes 589828
  0.7 98.1 %copy-start.2 = (f32[64,768]{1,0:T(8,128)S(1)}, f32[64,768]{1,0:T(8,128)}, u32[]{:S(2)}) copy-start(f32[64,768]{1,0:T(8,128)} %param.9) | copy-start | bytes 589828
